TPU v7x, 256 devices: a whole 4x4x8 slice. The times are simulated.
256 devices in a mesh: dir: 8 (over x, core), surf: 32 (over y, z).
Axes of the slice: x: 4, y: 4, z: 8, core: 2. Of those that a mesh axis runs over, the one named last changes fastest.
Arguments:
- direction_angles: float32 [2, 32768], P(None, 'dir'), may hold values from -3.140625 to 3.140625
- positions: float32 [3, 24576], P(None, 'surf'), may hold values from -12 to 12
- normal_angles: float32 [2, 24576], P(None, 'surf'), may hold values from -3.140625 to 3.140625
- areas: float32 [24576], P('surf'), may hold values from 0.5 to 2
- pressure: bfloat16 [24576, 128], P('surf'), may hold values from -6 to 6
- velocity: bfloat16 [24576, 128], P('surf'), may hold values from -6 to 6
- targets: float32 [32768, 64], P('dir'), may hold values from 0.5 to 3
Outputs:
- responses: float32 [32768, 128], P(('dir', 'surf'))
- grad_pressure: float32 [24576, 128], P('surf')
- grad_velocity: float32 [24576, 128], P('surf')
All inputs are finite; a program needn't handle non-finite values.
Results may differ from a plain program's by a relative error of at most 0.0052.
Values may be sent and summed in bfloat16 or wider, within the bound.
A program may use at most 64 MiB of HBM per device.

v0:
```python
import math

import jax
import jax.numpy as jnp
from jax import lax
from jax.sharding import PartitionSpec as P

floor_value = 0.5


def unit_vectors(angles):
    polar = angles[0]
    azimuth = angles[1]
    return jnp.stack(
        [jnp.sin(polar) * jnp.cos(azimuth), jnp.sin(polar) * jnp.sin(azimuth), jnp.cos(polar)]
    )


def kernel_tile(toward, points, facing):
    phase_angle = (
        toward[0][:, None] * points[0][None, :]
        + toward[1][:, None] * points[1][None, :]
        + toward[2][:, None] * points[2][None, :]
    )
    alignment = (
        toward[0][:, None] * facing[0][None, :]
        + toward[1][:, None] * facing[1][None, :]
        + toward[2][:, None] * facing[2][None, :]
    )
    cosine = jnp.cos(phase_angle)
    sine_part = jnp.sin(phase_angle)
    return jnp.concatenate(
        [
            cosine.astype(jnp.bfloat16),
            (-sine_part).astype(jnp.bfloat16),
            (cosine * alignment).astype(jnp.bfloat16),
            (-sine_part * alignment).astype(jnp.bfloat16),
        ],
        axis=1,
    )


def stacked_sources(weighted_v, weighted_p, cases):
    velocity_real = weighted_v[:, :cases]
    velocity_imag = weighted_v[:, cases:]
    pressure_real = weighted_p[:, :cases]
    pressure_imag = weighted_p[:, cases:]
    return jnp.concatenate(
        [
            weighted_v,
            jnp.concatenate([-velocity_imag, velocity_real], 1),
            weighted_p,
            jnp.concatenate([-pressure_imag, pressure_real], 1),
        ],
        0,
    )


def misfit_residual(responses, targets):
    cases = targets.shape[1]
    real_part = responses[:, :cases]
    imag_part = responses[:, cases:]
    magnitude = jnp.sqrt(real_part * real_part + imag_part * imag_part)
    weight = (magnitude - targets) / jnp.maximum(magnitude, floor_value)
    return jnp.concatenate([weight * real_part, weight * imag_part], 1).astype(jnp.bfloat16)


def combine_terms(products, scales, patch_rows, cases):
    mono_a = products[:patch_rows]
    mono_b = products[patch_rows : 2 * patch_rows]
    dip_a = products[2 * patch_rows : 3 * patch_rows]
    dip_b = products[3 * patch_rows :]
    mono_real = mono_a[:, :cases] + mono_b[:, cases:]
    mono_imag = mono_a[:, cases:] - mono_b[:, :cases]
    dip_real = dip_a[:, :cases] + dip_b[:, cases:]
    dip_imag = dip_a[:, cases:] - dip_b[:, :cases]
    column = scales[:, None]
    return jnp.concatenate(
        [column * dip_imag, -column * dip_real, column * mono_imag, -column * mono_real], 1
    )


def block_size():
    return 128


def flip_to_responses(totals, cases):
    return jnp.concatenate([-totals[:, cases:], totals[:, :cases]], 1)


def shards(direction_angles, positions, normal_angles, areas, pressure, velocity, targets):
    cases = targets.shape[1]
    patch_count = positions.shape[1]
    dir_count = direction_angles.shape[1]
    total_patches = patch_count * lax.axis_size("surf")
    toward = unit_vectors(direction_angles)
    facing = unit_vectors(normal_angles)
    scales = areas * jnp.float32(1.0 / math.sqrt(total_patches))
    weighted_p = (pressure.astype(jnp.float32) * scales[:, None]).astype(jnp.bfloat16)
    weighted_v = (velocity.astype(jnp.float32) * scales[:, None]).astype(jnp.bfloat16)
    block_rows = block_size()

    def forward_step(running, block_index):
        begin = block_index * block_rows
        points = lax.dynamic_slice_in_dim(positions, begin, block_rows, 1)
        normal_rows = lax.dynamic_slice_in_dim(facing, begin, block_rows, 1)
        velo_rows = lax.dynamic_slice_in_dim(weighted_v, begin, block_rows, 0)
        press_rows = lax.dynamic_slice_in_dim(weighted_p, begin, block_rows, 0)
        kernel = kernel_tile(toward, points, normal_rows)
        stacked = stacked_sources(velo_rows, press_rows, cases)
        return (running + jnp.dot(kernel, stacked, preferred_element_type=jnp.float32), None)

    initial = jnp.zeros((dir_count, 2 * cases), jnp.float32)
    forward, unused = lax.scan(
        forward_step, initial, jnp.arange(patch_count // block_rows, dtype=jnp.int32)
    )
    surf_count = lax.axis_size("surf")
    share_rows = dir_count // surf_count
    surf_index = lax.axis_index("surf")
    totals = lax.psum(forward, "surf")
    full_responses = flip_to_responses(totals, cases)
    responses = lax.dynamic_slice_in_dim(full_responses, surf_index * share_rows, share_rows, 0)
    residual = misfit_residual(full_responses, targets)
    rows_each = block_size()

    def one_block(block_index):
        begin = 0 + block_index * rows_each
        points = lax.dynamic_slice_in_dim(positions, begin, rows_each, 1)
        normal_rows = lax.dynamic_slice_in_dim(facing, begin, rows_each, 1)
        scale_rows = lax.dynamic_slice_in_dim(scales, begin, rows_each, 0)
        kernel = kernel_tile(toward, points, normal_rows)
        products = lax.dot_general(
            kernel, residual, (((0,), (0,)), ((), ())), preferred_element_type=jnp.float32
        )
        return combine_terms(products, scale_rows, rows_each, cases)

    blocks = lax.map(one_block, jnp.arange(patch_count // rows_each, dtype=jnp.int32))
    gradients = lax.psum(blocks.reshape(patch_count, 4 * cases), "dir")
    return (responses, gradients[:, : 2 * cases], gradients[:, 2 * cases :])


def solution(mesh):
    in_specs = (
        P(None, "dir"),
        P(None, "surf"),
        P(None, "surf"),
        P("surf"),
        P("surf", None),
        P("surf", None),
        P("dir", None),
    )
    out_specs = (P(("dir", "surf"), None), P("surf", None), P("surf", None))
    return jax.shard_map(shards, mesh=mesh, in_specs=in_specs, out_specs=out_specs, check_vma=False)
```

profile of v0, /device:TPU:1, one launch (start us, length us, event | category | flops | bytes accessed | tf_op | source)
XLA Modules:
  0.0 446.0 jit_solution(15041724441343652685)
XLA Ops:
  8.2 2.4 slice_cosine_fusion
  13.6 115.3 %while.22 = (s32[]{:T(128)}, f32[4096,128]{1,0:T(8,128)}, f32[4096]{0:T(1024)}, s32[6]{0:T(128)}, f32[3,768]{1,0:T(4,128)}, /*index=5*/f32[4096]{0:T(1024)}, f32...) while((s32[]{:T(128)}, f32[4096,128]{1,0:T(8,128)}, ...), condition=%wide.region_1.2_spmd.clone, body=%wide.region_0.1_spmd.clone.sunk | while | flops 564445184 | bytes 13040877 | solution.py:114
  16.3 10.7 %fusion.59 = (bf16[4096,128]{1,0:T(8,128)(2,1)S(1)}, bf16[4096,128]{1,0:T(8,128)(2,1)S(1)}, bf16[4096,128]{1,0:T(8,128)(2,1)S(1)}, bf16[4096,128]{1,0:T(8,128)(2,1)}) fusion(f32[128]{0:T(128)S(1)} %get-tuple-element.430, f32[4096]{0:T(1024)S(1)} %get-tuple-element.483, f32[128]{0:T(128)S(1)} %get-tuple-element.431, f32[4096]{0:T(1024)} %get-tuple-element.482, ...), kind=kLoop, calls=%fused_computation.49.clone.1 | loop fusion | flops 8912896 | bytes 4246528 | tf_op jit(solution)/shard_map/while/body/eval_jaxpr/convert_element_type | solution.py:34
  28.3 3.9 convolution_add_fusion.2
  34.8 10.7 %fusion.59 = (bf16[4096,128]{1,0:T(8,128)(2,1)S(1)}, bf16[4096,128]{1,0:T(8,128)(2,1)S(1)}, bf16[4096,128]{1,0:T(8,128)(2,1)S(1)}, bf16[4096,128]{1,0:T(8,128)(2,1)}) fusion(f32[128]{0:T(128)S(1)} %get-tuple-element.430, f32[4096]{0:T(1024)S(1)} %get-tuple-element.483, f32[128]{0:T(128)S(1)} %get-tuple-element.431, f32[4096]{0:T(1024)} %get-tuple-element.482, ...), kind=kLoop, calls=%fused_computation.49.clone.1 | loop fusion | flops 8912896 | bytes 4246528 | tf_op jit(solution)/shard_map/while/body/eval_jaxpr/convert_element_type | solution.py:34
  46.9 4.7 %convolution_add_fusion.2 = f32[4096,128]{1,0:T(8,128)} fusion(bf16[4096,128]{1,0:T(8,128)(2,1)S(1)} %get-tuple-element.437, bf16[4096,128]{1,0:T(8,128)(2,1)} %get-tuple-element.438, bf16[4096,128]{1,0:T(8,128)(2,1)S(1)} %get-tuple-element.439, bf16[4096,128]{1,0:T(8,128)(2,1)S(1)} %get-tuple-element.440, f32[4096,128]{1,0:T(8,128)} %get-tuple-element.463, ...), kind=kOutput, calls=%fused_computation.35.clone.1 | convolution fusion | flops 555483136 | bytes 8519681 | tf_op jit(solution)/shard_map/while/body/eval_jaxpr/dot_general | solution.py:111
  54.2 10.7 %fusion.59 = (bf16[4096,128]{1,0:T(8,128)(2,1)S(1)}, bf16[4096,128]{1,0:T(8,128)(2,1)S(1)}, bf16[4096,128]{1,0:T(8,128)(2,1)S(1)}, bf16[4096,128]{1,0:T(8,128)(2,1)}) fusion(f32[128]{0:T(128)S(1)} %get-tuple-element.430, f32[4096]{0:T(1024)S(1)} %get-tuple-element.483, f32[128]{0:T(128)S(1)} %get-tuple-element.431, f32[4096]{0:T(1024)} %get-tuple-element.482, ...), kind=kLoop, calls=%fused_computation.49.clone.1 | loop fusion | flops 8912896 | bytes 4246528 | tf_op jit(solution)/shard_map/while/body/eval_jaxpr/convert_element_type | solution.py:34
  66.2 4.7 %convolution_add_fusion.2 = f32[4096,128]{1,0:T(8,128)} fusion(bf16[4096,128]{1,0:T(8,128)(2,1)S(1)} %get-tuple-element.437, bf16[4096,128]{1,0:T(8,128)(2,1)} %get-tuple-element.438, bf16[4096,128]{1,0:T(8,128)(2,1)S(1)} %get-tuple-element.439, bf16[4096,128]{1,0:T(8,128)(2,1)S(1)} %get-tuple-element.440, f32[4096,128]{1,0:T(8,128)} %get-tuple-element.463, ...), kind=kOutput, calls=%fused_computation.35.clone.1 | convolution fusion | flops 555483136 | bytes 8519681 | tf_op jit(solution)/shard_map/while/body/eval_jaxpr/dot_general | solution.py:111
  73.5 10.7 %fusion.59 = (bf16[4096,128]{1,0:T(8,128)(2,1)S(1)}, bf16[4096,128]{1,0:T(8,128)(2,1)S(1)}, bf16[4096,128]{1,0:T(8,128)(2,1)S(1)}, bf16[4096,128]{1,0:T(8,128)(2,1)}) fusion(f32[128]{0:T(128)S(1)} %get-tuple-element.430, f32[4096]{0:T(1024)S(1)} %get-tuple-element.483, f32[128]{0:T(128)S(1)} %get-tuple-element.431, f32[4096]{0:T(1024)} %get-tuple-element.482, ...), kind=kLoop, calls=%fused_computation.49.clone.1 | loop fusion | flops 8912896 | bytes 4246528 | tf_op jit(solution)/shard_map/while/body/eval_jaxpr/convert_element_type | solution.py:34
  85.6 4.7 %convolution_add_fusion.2 = f32[4096,128]{1,0:T(8,128)} fusion(bf16[4096,128]{1,0:T(8,128)(2,1)S(1)} %get-tuple-element.437, bf16[4096,128]{1,0:T(8,128)(2,1)} %get-tuple-element.438, bf16[4096,128]{1,0:T(8,128)(2,1)S(1)} %get-tuple-element.439, bf16[4096,128]{1,0:T(8,128)(2,1)S(1)} %get-tuple-element.440, f32[4096,128]{1,0:T(8,128)} %get-tuple-element.463, ...), kind=kOutput, calls=%fused_computation.35.clone.1 | convolution fusion | flops 555483136 | bytes 8519681 | tf_op jit(solution)/shard_map/while/body/eval_jaxpr/dot_general | solution.py:111
  92.9 10.7 %fusion.59 = (bf16[4096,128]{1,0:T(8,128)(2,1)S(1)}, bf16[4096,128]{1,0:T(8,128)(2,1)S(1)}, bf16[4096,128]{1,0:T(8,128)(2,1)S(1)}, bf16[4096,128]{1,0:T(8,128)(2,1)}) fusion(f32[128]{0:T(128)S(1)} %get-tuple-element.430, f32[4096]{0:T(1024)S(1)} %get-tuple-element.483, f32[128]{0:T(128)S(1)} %get-tuple-element.431, f32[4096]{0:T(1024)} %get-tuple-element.482, ...), kind=kLoop, calls=%fused_computation.49.clone.1 | loop fusion | flops 8912896 | bytes 4246528 | tf_op jit(solution)/shard_map/while/body/eval_jaxpr/convert_element_type | solution.py:34
  104.9 4.7 %convolution_add_fusion.2 = f32[4096,128]{1,0:T(8,128)} fusion(bf16[4096,128]{1,0:T(8,128)(2,1)S(1)} %get-tuple-element.437, bf16[4096,128]{1,0:T(8,128)(2,1)} %get-tuple-element.438, bf16[4096,128]{1,0:T(8,128)(2,1)S(1)} %get-tuple-element.439, bf16[4096,128]{1,0:T(8,128)(2,1)S(1)} %get-tuple-element.440, f32[4096,128]{1,0:T(8,128)} %get-tuple-element.463, ...), kind=kOutput, calls=%fused_computation.35.clone.1 | convolution fusion | flops 555483136 | bytes 8519681 | tf_op jit(solution)/shard_map/while/body/eval_jaxpr/dot_general | solution.py:111
  112.2 10.7 %fusion.59 = (bf16[4096,128]{1,0:T(8,128)(2,1)S(1)}, bf16[4096,128]{1,0:T(8,128)(2,1)S(1)}, bf16[4096,128]{1,0:T(8,128)(2,1)S(1)}, bf16[4096,128]{1,0:T(8,128)(2,1)}) fusion(f32[128]{0:T(128)S(1)} %get-tuple-element.430, f32[4096]{0:T(1024)S(1)} %get-tuple-element.483, f32[128]{0:T(128)S(1)} %get-tuple-element.431, f32[4096]{0:T(1024)} %get-tuple-element.482, ...), kind=kLoop, calls=%fused_computation.49.clone.1 | loop fusion | flops 8912896 | bytes 4246528 | tf_op jit(solution)/shard_map/while/body/eval_jaxpr/convert_element_type | solution.py:34
  124.3 4.7 %convolution_add_fusion.2 = f32[4096,128]{1,0:T(8,128)} fusion(bf16[4096,128]{1,0:T(8,128)(2,1)S(1)} %get-tuple-element.437, bf16[4096,128]{1,0:T(8,128)(2,1)} %get-tuple-element.438, bf16[4096,128]{1,0:T(8,128)(2,1)S(1)} %get-tuple-element.439, bf16[4096,128]{1,0:T(8,128)(2,1)S(1)} %get-tuple-element.440, f32[4096,128]{1,0:T(8,128)} %get-tuple-element.463, ...), kind=kOutput, calls=%fused_computation.35.clone.1 | convolution fusion | flops 555483136 | bytes 8519681 | tf_op jit(solution)/shard_map/while/body/eval_jaxpr/dot_general | solution.py:111
  129.0 2.9 copy.12
  132.0 153.8 %all-reduce.3.cloned.1.call-done = f32[4096,128]{0,1:T(8,128)} async-done(((f32[4096,128]{0,1:T(8,128)}), f32[4096,128]{0,1:T(8,128)}) %all-reduce.3.cloned.1.call-update) | async-done | bytes 2097168 | tf_op jit(solution)/shard_map/psum | solution.py:120
  289.4 81.6 %while.21 = (s32[]{:T(128)}, f32[6,128,256]{2,1,0:T(8,128)}, s32[6]{0:T(128)S(1)}, f32[768]{0:T(1024)}, f32[4096]{0:T(1024)S(1)}, /*index=5*/f32[3,768]{1,0:T(4,...) while((s32[]{:T(128)}, f32[6,128,256]{2,1,0:T(8,128)}, ...), condition=%wide.region_4.5_spmd, body=%wide.region_3.4_spmd.sunk | while | flops 562724992 | bytes 15141091 | solution.py:137
  291.3 9.2 %fusion.53 = (bf16[4096,128]{1,0:T(8,128)(2,1)S(1)}, bf16[4096,128]{1,0:T(8,128)(2,1)S(1)}, bf16[4096,128]{1,0:T(8,128)(2,1)S(1)}, bf16[4096,128]{1,0:T(8,128)(2,1)S(1)}) fusion(f32[128]{0:T(128)S(1)} %get-tuple-element.402, f32[4096]{0:T(1024)S(1)} %get-tuple-element.527, f32[128]{0:T(128)S(1)} %get-tuple-element.403, ...), kind=kLoop, calls=%fused_computation.14.clone.1 | loop fusion | flops 8912896 | bytes 4246528 | tf_op jit(solution)/shard_map/while/body/eval_jaxpr/convert_element_type | solution.py:34
  304.9 9.2 %fusion.53 = (bf16[4096,128]{1,0:T(8,128)(2,1)S(1)}, bf16[4096,128]{1,0:T(8,128)(2,1)S(1)}, bf16[4096,128]{1,0:T(8,128)(2,1)S(1)}, bf16[4096,128]{1,0:T(8,128)(2,1)S(1)}) fusion(f32[128]{0:T(128)S(1)} %get-tuple-element.402, f32[4096]{0:T(1024)S(1)} %get-tuple-element.527, f32[128]{0:T(128)S(1)} %get-tuple-element.403, ...), kind=kLoop, calls=%fused_computation.14.clone.1 | loop fusion | flops 8912896 | bytes 4246528 | tf_op jit(solution)/shard_map/while/body/eval_jaxpr/convert_element_type | solution.py:34
  318.5 9.2 %fusion.53 = (bf16[4096,128]{1,0:T(8,128)(2,1)S(1)}, bf16[4096,128]{1,0:T(8,128)(2,1)S(1)}, bf16[4096,128]{1,0:T(8,128)(2,1)S(1)}, bf16[4096,128]{1,0:T(8,128)(2,1)S(1)}) fusion(f32[128]{0:T(128)S(1)} %get-tuple-element.402, f32[4096]{0:T(1024)S(1)} %get-tuple-element.527, f32[128]{0:T(128)S(1)} %get-tuple-element.403, ...), kind=kLoop, calls=%fused_computation.14.clone.1 | loop fusion | flops 8912896 | bytes 4246528 | tf_op jit(solution)/shard_map/while/body/eval_jaxpr/convert_element_type | solution.py:34
  332.1 9.2 %fusion.53 = (bf16[4096,128]{1,0:T(8,128)(2,1)S(1)}, bf16[4096,128]{1,0:T(8,128)(2,1)S(1)}, bf16[4096,128]{1,0:T(8,128)(2,1)S(1)}, bf16[4096,128]{1,0:T(8,128)(2,1)S(1)}) fusion(f32[128]{0:T(128)S(1)} %get-tuple-element.402, f32[4096]{0:T(1024)S(1)} %get-tuple-element.527, f32[128]{0:T(128)S(1)} %get-tuple-element.403, ...), kind=kLoop, calls=%fused_computation.14.clone.1 | loop fusion | flops 8912896 | bytes 4246528 | tf_op jit(solution)/shard_map/while/body/eval_jaxpr/convert_element_type | solution.py:34
  345.7 9.2 %fusion.53 = (bf16[4096,128]{1,0:T(8,128)(2,1)S(1)}, bf16[4096,128]{1,0:T(8,128)(2,1)S(1)}, bf16[4096,128]{1,0:T(8,128)(2,1)S(1)}, bf16[4096,128]{1,0:T(8,128)(2,1)S(1)}) fusion(f32[128]{0:T(128)S(1)} %get-tuple-element.402, f32[4096]{0:T(1024)S(1)} %get-tuple-element.527, f32[128]{0:T(128)S(1)} %get-tuple-element.403, ...), kind=kLoop, calls=%fused_computation.14.clone.1 | loop fusion | flops 8912896 | bytes 4246528 | tf_op jit(solution)/shard_map/while/body/eval_jaxpr/convert_element_type | solution.py:34
  359.3 9.2 %fusion.53 = (bf16[4096,128]{1,0:T(8,128)(2,1)S(1)}, bf16[4096,128]{1,0:T(8,128)(2,1)S(1)}, bf16[4096,128]{1,0:T(8,128)(2,1)S(1)}, bf16[4096,128]{1,0:T(8,128)(2,1)S(1)}) fusion(f32[128]{0:T(128)S(1)} %get-tuple-element.402, f32[4096]{0:T(1024)S(1)} %get-tuple-element.527, f32[128]{0:T(128)S(1)} %get-tuple-element.403, ...), kind=kLoop, calls=%fused_computation.14.clone.1 | loop fusion | flops 8912896 | bytes 4246528 | tf_op jit(solution)/shard_map/while/body/eval_jaxpr/convert_element_type | solution.py:34
  371.7 65.4 %all-reduce.5.cloned.1.call-done = f32[768,256]{1,0:T(8,128)} async-done(((f32[768,256]{1,0:T(8,128)}), f32[768,256]{1,0:T(8,128)}) %all-reduce.5.cloned.1.call-update) | async-done | bytes 786448 | tf_op jit(solution)/shard_map/psum | solution.py:138
  (134 shorter events, 52.3 us)
Async XLA Ops:
  7.2 278.6 %all-reduce.3.cloned.1.call-start = ((), (), s32[]{:S(2)}) async-start(), calls=%async_computation | async-start | bytes 4194304 | tf_op jit(solution)/shard_map/psum | solution.py:120
  11.2 2.4 copy-start.4
  131.9 153.9 %copy-start.3 = (f32[4096,64]{0,1:T(8,128)S(1)}, f32[4096,64]{0,1:T(8,128)}, u32[]{:S(2)}) copy-start(f32[4096,64]{0,1:T(8,128)} %param.17) | copy-start | bytes 3145732
  131.9 305.2 %all-reduce.5.cloned.1.call-start = ((), (), s32[]{:S(2)}) async-start(), calls=%async_computation.1 | async-start | bytes 1572864 | tf_op jit(solution)/shard_map/psum | solution.py:138
  287.9 1.4 copy-start
  288.0 1.4 copy-start.1
  291.3 9.2 %copy-start.2 = (bf16[4096,128]{1,0:T(8,128)(2,1)S(1)}, bf16[4096,128]{1,0:T(8,128)(2,1)}, u32[]{:S(2)}) copy-start(bf16[4096,128]{1,0:T(8,128)(2,1)} %get-tuple-element.529) | copy-start | bytes 3145732 | tf_op jit(solution)/shard_map/while
  304.9 9.2 %copy-start.2 = (bf16[4096,128]{1,0:T(8,128)(2,1)S(1)}, bf16[4096,128]{1,0:T(8,128)(2,1)}, u32[]{:S(2)}) copy-start(bf16[4096,128]{1,0:T(8,128)(2,1)} %get-tuple-element.529) | copy-start | bytes 3145732 | tf_op jit(solution)/shard_map/while
  318.5 9.2 %copy-start.2 = (bf16[4096,128]{1,0:T(8,128)(2,1)S(1)}, bf16[4096,128]{1,0:T(8,128)(2,1)}, u32[]{:S(2)}) copy-start(bf16[4096,128]{1,0:T(8,128)(2,1)} %get-tuple-element.529) | copy-start | bytes 3145732 | tf_op jit(solution)/shard_map/while
  332.1 9.2 %copy-start.2 = (bf16[4096,128]{1,0:T(8,128)(2,1)S(1)}, bf16[4096,128]{1,0:T(8,128)(2,1)}, u32[]{:S(2)}) copy-start(bf16[4096,128]{1,0:T(8,128)(2,1)} %get-tuple-element.529) | copy-start | bytes 3145732 | tf_op jit(solution)/shard_map/while
  345.7 9.2 %copy-start.2 = (bf16[4096,128]{1,0:T(8,128)(2,1)S(1)}, bf16[4096,128]{1,0:T(8,128)(2,1)}, u32[]{:S(2)}) copy-start(bf16[4096,128]{1,0:T(8,128)(2,1)} %get-tuple-element.529) | copy-start | bytes 3145732 | tf_op jit(solution)/shard_map/while
  359.3 9.2 %copy-start.2 = (bf16[4096,128]{1,0:T(8,128)(2,1)S(1)}, bf16[4096,128]{1,0:T(8,128)(2,1)}, u32[]{:S(2)}) copy-start(bf16[4096,128]{1,0:T(8,128)(2,1)} %get-tuple-element.529) | copy-start | bytes 3145732 | tf_op jit(solution)/shard_map/while
Sparse Core Ops, SparseCore 0:
  132.0 153.6 all-reduce.2
  371.1 66.0 all-reduce.4
where the time goes:
time: 449 us; the launch traced here: 446 us
  waiting for transfers between devices  219 us (49%)
  other arithmetic  137 us (31%)
  local copies, waits for them, and re-layouts  35.4 us (8%)
  matrix products  32.2 us (7%)
  between operations  14.1 us (3%)
  loops' own time  8.22 us (2%)
    psum x1, waiting for transfers between devices, shards(): totals = lax.psum(forward, 'surf')  154 us
    convert_element_type x12, other arithmetic, kernel_tile(): cosine.astype(jnp.bfloat16)  120 us
    psum x1, waiting for transfers between devices, shards(): gradients = lax.psum(blocks.reshape(patch_count, 4 * cases), 'dir')  65.4 us
    dot_general x6, matrix products, forward_step(): jnp.dot(kernel, stacked, preferred_element_type=jnp.float32)  27.3 us
    dynamic_slice x12, local copies, waits for them, and re-layouts, shards(): lax.scan(forward_step, initial, jnp.arange(patch_count // block_rows, dty...  11.1 us
  transfers between devices with their start and end apart: 2, of which 2 were waited for; matrix products, arithmetic and copies ran while one was open for 0% of the time, Pallas kernels for 0%

commit v1 on v0

v1 whole, which is shorter than its diff:
```python
import functools
import math

import jax
import jax.numpy as jnp
from jax import lax
from jax.experimental import pallas as pl
from jax.experimental.pallas import tpu as pltpu
from jax.sharding import PartitionSpec as P

MESH = pl.DeviceIdType.MESH
BF = jnp.bfloat16
F32 = jnp.float32
FLOOR = 0.5

TILES = 4
NY, NZ, NX = 4, 8, 4
OWN = 32
SUB = NZ * OWN
ROWS = NY * SUB
DELTAS = (2, 1, 3, 0)
SLOT_OF_SEND = {1: 2, 2: 0, 3: 1}

ROOT2 = math.sqrt(2.0)
SIN_HALF = [c * ROOT2 for c in (3.14158198, -5.1671413, 2.54188707, -0.55460885)]
COS_HALF = [c * ROOT2 for c in (0.99999325, -4.93393467, 4.0412481, -1.22203176)]
SIN_FINE = [c * ROOT2 for c in (3.14159258, -5.16770687, 2.55003119, -0.59804419, 0.07721839)]
COS_FINE = [c * ROOT2 for c in (0.99999995, -4.93479283, 4.05841135, -1.33187657, 0.21968961)]


def horner(coefficients, square):
    value = coefficients[-1]
    for coefficient in coefficients[-2::-1]:
        value = value * square + coefficient
    return value


def cos_sin(cycles, sin_half, cos_half):
    rest = cycles - jnp.round(cycles)
    square = rest * rest
    half_sine = horner(sin_half, square) * rest
    half_cosine = horner(cos_half, square)
    return 1.0 - half_sine * half_sine, half_sine * half_cosine


def fine_cos_sin(angle):
    return cos_sin(angle * F32(1.0 / (2.0 * math.pi)), SIN_FINE, COS_FINE)


def unit_rows(angles):
    cos_all, sin_all = fine_cos_sin(angles)
    cos_polar, sin_polar = cos_all[0:1], sin_all[0:1]
    cos_azimuth, sin_azimuth = cos_all[1:2], sin_all[1:2]
    return sin_polar * cos_azimuth, sin_polar * sin_azimuth, cos_polar


def three_parts(value):
    first = value.astype(BF).astype(F32)
    second = (value - first).astype(BF).astype(F32)
    return first, second, value - first - second


def body(
    total_patches,
    angles_ref, positions_ref, normals_ref, areas_ref, pressure_ref, velocity_ref, targets_hbm,
    responses_ref, grad_p_ref, grad_v_ref,
    targets_ref, split_t, split_x, t_rows, t_cols, t_lhs, x_rhs, face_rows, weights,
    cos_a, sin_a, cos_b, sin_b,
    part_send, part_own, part_recv, row_own, row_send, row_recv, res_all, acc,
    half_send, half_recv, quarter_own, quarter_send, quarter_recv, grad_all,
    local_sem, a_send, a_recv, b_send, b_recv, d_send, d_recv, e_send, e_recv,
    g_send, g_recv, h_send, h_recv, k_send, k_recv,
):
    dir_index = lax.axis_index("dir")
    surf_index = lax.axis_index("surf")
    x, core = dir_index // 2, lax.rem(dir_index, 2)
    y, z = surf_index // NZ, lax.rem(surf_index, NZ)
    patches = positions_ref.shape[1]

    def at_y(e):
        return (dir_index, lax.rem(y + e, NY) * NZ + z)

    def at_z(e):
        return (dir_index, y * NZ + lax.rem(z + e, NZ))

    def at_dir(ex, ec):
        return (lax.rem(x + ex, NX) * 2 + lax.rem(core + ec, 2), surf_index)

    group = [(ex, ec) for ex in range(NX) for ec in range(2) if ex or ec]
    barrier = pltpu.get_barrier_semaphore()
    for e in range(1, NY):
        pl.semaphore_signal(barrier, inc=1, device_id=at_y(e), device_id_type=MESH)
    for e in range(1, NZ):
        pl.semaphore_signal(barrier, inc=1, device_id=at_z(e), device_id_type=MESH)
    for ex, ec in group:
        pl.semaphore_signal(barrier, inc=1, device_id=at_dir(ex, ec), device_id_type=MESH)

    own_rows = TILES * OWN
    fetch = pltpu.make_async_copy(
        targets_hbm.at[pl.ds(pl.multiple_of(surf_index * own_rows, own_rows), own_rows)],
        targets_ref, local_sem,
    )
    fetch.start()

    tx, ty, tz = unit_rows(angles_ref[...])
    split_t[...] = jnp.zeros_like(split_t)
    split_x[...] = jnp.zeros_like(split_x)
    t_rows[...] = jnp.zeros_like(t_rows)
    for k, row in enumerate((tx, ty, tz)):
        t_rows[k : k + 1, :] = row
        first, second, third = three_parts(row)
        for at, part in enumerate((first, first, second, second, first, third)):
            split_t[3 * at + k : 3 * at + k + 1, :] = part
        first, second, third = three_parts(positions_ref[k : k + 1, :] * F32(0.5 / math.pi))
        for at, part in enumerate((first, second, first, second, third, first)):
            split_x[3 * at + k : 3 * at + k + 1, :] = part
    x_rhs[...] = split_x[...].astype(BF)
    t_lhs[...] = split_t[...].T.astype(BF)
    t_cols[...] = t_rows[...].T

    face_rows[...] = jnp.zeros_like(face_rows)
    scale_row = areas_ref[...] * F32(1.0 / math.sqrt(total_patches))
    for k, row in enumerate(unit_rows(normals_ref[...])):
        face_rows[k : k + 1, :] = row
    face_rows[3:4, :] = scale_row
    face_cols = face_rows[...].T
    scale_col = face_cols[:, 3:4]
    weighted_p = (pressure_ref[...].astype(F32) * scale_col).astype(BF).astype(F32)
    weighted_v = (velocity_ref[...].astype(F32) * scale_col).astype(BF).astype(F32)
    cases = weighted_p.shape[1] // 2
    for k in range(4):
        source = weighted_v if k == 0 else weighted_p * face_cols[:, k - 1 : k]
        turned = jnp.concatenate([source[:, cases:], -source[:, :cases]], axis=1)
        columns = slice(k * 2 * cases, (k + 1) * 2 * cases)
        weights[0:patches, columns] = source.astype(BF)
        weights[patches : 2 * patches, columns] = turned.astype(BF)
    acc[...] = jnp.zeros_like(acc)

    def sub_row(q, j):
        return pl.multiple_of(q * ROWS + lax.rem(y + DELTAS[j], NY) * SUB, SUB)

    def trig_piece(q, j, cos_ref, sin_ref, slot, begin, count):
        angle = jnp.dot(
            t_lhs[pl.ds(sub_row(q, j) + begin, count), :], x_rhs[...], preferred_element_type=F32
        )
        cosine, sine = cos_sin(angle, SIN_HALF, COS_HALF)
        at = pl.multiple_of(slot * SUB + begin, count)
        cos_ref[pl.ds(at, count), :] = cosine.astype(BF)
        sin_ref[pl.ds(at, count), :] = sine.astype(BF)

    quarter = SUB // 4

    def forward_step(tq, tj, tslot, mq, mj, mslot):
        tc, ts = (cos_a, sin_a) if tj % 2 == 0 else (cos_b, sin_b)
        mc, ms = (cos_a, sin_a) if mj % 2 == 0 else (cos_b, sin_b)
        rows = pl.ds(pl.multiple_of(mslot * SUB, SUB), SUB)
        halves = []
        for h in range(2):
            columns = slice(4 * cases * h, 4 * cases * (h + 1))
            g = jnp.dot(mc[rows, :], weights[0:patches, columns], preferred_element_type=F32)
            trig_piece(tq, tj, tc, ts, tslot, 2 * h * quarter, quarter)
            g = g + jnp.dot(
                ms[rows, :], weights[patches : 2 * patches, columns], preferred_element_type=F32
            )
            trig_piece(tq, tj, tc, ts, tslot, (2 * h + 1) * quarter, quarter)
            halves.append(g)
        t_at = t_cols[pl.ds(sub_row(mq, mj), SUB), :]
        lo, hi = halves
        return (
            lo[:, : 2 * cases]
            + t_at[:, 0:1] * lo[:, 2 * cases :]
            + t_at[:, 1:2] * hi[:, : 2 * cases]
            + t_at[:, 2:3] * hi[:, 2 * cases :]
        )

    def a_copy(q, e):
        at = pl.multiple_of((q * (NY - 1) + e - 1) * SUB, SUB)
        return pltpu.make_async_remote_copy(
            src_ref=part_send.at[pl.ds(at, SUB)], dst_ref=part_recv.at[pl.ds(at, SUB)],
            send_sem=a_send.at[q * (NY - 1) + e - 1], recv_sem=a_recv.at[q * (NY - 1) + e - 1],
            device_id=at_y(e), device_id_type=MESH,
        )

    def b_copy(q, e):
        return pltpu.make_async_remote_copy(
            src_ref=row_send.at[pl.ds(pl.multiple_of(q * SUB + lax.rem(z + e, NZ) * OWN, OWN), OWN)],
            dst_ref=row_recv.at[pl.ds(pl.multiple_of((q * (NZ - 1) + e - 1) * OWN, OWN), OWN)],
            send_sem=b_send.at[q * (NZ - 1) + e - 1], recv_sem=b_recv.at[q * (NZ - 1) + e - 1],
            device_id=at_z(e), device_id_type=MESH,
        )

    def d_copy(q, e, came=False):
        source = lax.rem(z + NZ - e, NZ) if came else z
        rows = pl.ds(pl.multiple_of(q * ROWS + 3 * SUB + source * OWN, OWN), OWN)
        return pltpu.make_async_remote_copy(
            src_ref=res_all.at[rows], dst_ref=res_all.at[rows],
            send_sem=d_send.at[q * (NZ - 1) + e - 1], recv_sem=d_recv.at[q * (NZ - 1) + e - 1],
            device_id=at_z(e), device_id_type=MESH,
        )

    def e_copy(q, e):
        return pltpu.make_async_remote_copy(
            src_ref=res_all.at[pl.ds(pl.multiple_of(q * ROWS + 3 * SUB, SUB), SUB)],
            dst_ref=res_all.at[pl.ds(pl.multiple_of(q * ROWS + SLOT_OF_SEND[e] * SUB, SUB), SUB)],
            send_sem=e_send.at[q * (NY - 1) + e - 1], recv_sem=e_recv.at[q * (NY - 1) + e - 1],
            device_id=at_y(e), device_id_type=MESH,
        )

    def send_part(q, j, partial):
        e = DELTAS[j]
        at = pl.multiple_of((q * (NY - 1) + e - 1) * SUB, SUB)
        part_send[pl.ds(at, SUB), :] = partial.astype(BF)
        a_copy(q, e).start()

    def forward_tile(q):
        send_part(q, 0, forward_step(q, 1, 2 * q, q, 0, 2 * q))
        send_part(q, 1, forward_step(q, 2, 2 * q + 1, q, 1, 2 * q))
        send_part(q, 2, forward_step(q, 3, 2 * q + 1, q, 2, 2 * q + 1))
        after = lax.rem(q + 1, TILES)
        own = forward_step(after, 0, 2 * q + 2, q, 3, 2 * q + 1)
        part_own[pl.ds(pl.multiple_of(q * SUB, SUB), SUB), :] = own

    def sum_over_y(q):
        rows = pl.ds(pl.multiple_of(q * SUB, SUB), SUB)
        total = part_own[rows, :]
        for e in range(1, NY):
            a_copy(q, e).wait_recv()
        for e in range(1, NY):
            at = pl.multiple_of((q * (NY - 1) + e - 1) * SUB, SUB)
            total = total + part_recv[pl.ds(at, SUB), :].astype(F32)
        row_own[rows, :] = total
        row_send[rows, :] = total.astype(BF)
        for e in range(1, NZ):
            b_copy(q, e).start()

    def make_residual(q):
        total = row_own[pl.ds(pl.multiple_of(q * SUB + z * OWN, OWN), OWN), :]
        for e in range(1, NZ):
            b_copy(q, e).wait_recv()
        for e in range(1, NZ):
            at = pl.multiple_of((q * (NZ - 1) + e - 1) * OWN, OWN)
            total = total + row_recv[pl.ds(at, OWN), :].astype(F32)
        real, imag = -total[:, cases:], total[:, :cases]
        out_rows = pl.ds(pl.multiple_of(q * OWN, OWN), OWN)
        responses_ref[out_rows, :] = jnp.concatenate([real, imag], axis=1)
        magnitude = jnp.sqrt(real * real + imag * imag)
        weight = (magnitude - targets_ref[out_rows, :]) / jnp.maximum(magnitude, FLOOR)
        residual = jnp.concatenate([weight * real, weight * imag], axis=1).astype(BF)
        res_all[pl.ds(pl.multiple_of(q * ROWS + 3 * SUB + z * OWN, OWN), OWN), :] = residual
        for e in range(1, NZ):
            d_copy(q, e).start()

    def share_over_y(q):
        for e in range(1, NZ):
            d_copy(q, e, came=True).wait_recv()
        for e in range(1, NY):
            e_copy(q, e).start()

    def adjoint_tile(q):
        for e in range(1, NY):
            e_copy(q, e).wait_recv()
        for parity, (cos_ref, sin_ref) in enumerate(((cos_a, sin_a), (cos_b, sin_b))):
            pieces, t_pieces = [], []
            for j in (parity, parity + 2):
                at = pl.multiple_of(q * ROWS + j * SUB, SUB)
                pieces.append(res_all[pl.ds(at, SUB), :].astype(F32))
                t_pieces.append(t_rows[:, pl.ds(sub_row(q, j), SUB)])
            turned = jnp.concatenate(pieces, axis=0).T
            t_at = jnp.concatenate(t_pieces, axis=1)
            swapped = jnp.concatenate([turned[cases:], -turned[:cases]], axis=0)
            with_cos, with_sin = [swapped.astype(BF)], [turned.astype(BF)]
            for k in range(3):
                with_cos.append((swapped * t_at[k : k + 1, :]).astype(BF))
                with_sin.append((turned * t_at[k : k + 1, :]).astype(BF))
            rows = pl.ds(pl.multiple_of(q * 2 * SUB, 2 * SUB), 2 * SUB)
            acc[...] += jnp.dot(
                jnp.concatenate(with_cos, axis=0), cos_ref[rows, :], preferred_element_type=F32
            ) + jnp.dot(
                jnp.concatenate(with_sin, axis=0), sin_ref[rows, :], preferred_element_type=F32
            )

    for begin in range(0, SUB, quarter):
        trig_piece(0, 0, cos_a, sin_a, 0, begin, quarter)
    fetch.wait()
    pl.semaphore_wait(barrier, (NY - 1) + (NZ - 1) + len(group))

    def step(it, carry):
        pl.when(it < TILES)(lambda: forward_tile(it))
        pl.when(it >= 4)(lambda: adjoint_tile(it - 4))
        pl.when(jnp.logical_and(it >= 3, it < TILES + 3))(lambda: share_over_y(it - 3))
        pl.when(jnp.logical_and(it >= 2, it < TILES + 2))(lambda: make_residual(it - 2))
        pl.when(jnp.logical_and(it >= 1, it < TILES + 1))(lambda: sum_over_y(it - 1))
        return carry

    lax.fori_loop(0, TILES + 4, step, 0)

    half = 2 * cases

    def gradient(which):
        if which == 0:
            return acc[0:half, :] * scale_row
        total = acc[half : 2 * half, :] * face_rows[0:1, :]
        for k in range(1, 3):
            total = total + acc[(k + 1) * half : (k + 2) * half, :] * face_rows[k : k + 1, :]
        return total * scale_row

    for which in range(2):
        grad = gradient(which)

        @pl.when(core == which)
        def _():
            quarter_own[...] = grad

        @pl.when(core != which)
        def _():
            half_send[...] = grad.astype(BF)

    g_copy = pltpu.make_async_remote_copy(
        src_ref=half_send, dst_ref=half_recv, send_sem=g_send, recv_sem=g_recv,
        device_id=at_dir(0, 1), device_id_type=MESH,
    )
    g_copy.start()
    g_copy.wait()
    chip = quarter_own[...] + half_recv[...].astype(F32)
    quarter_own[...] = chip
    quarter_send[...] = chip.astype(BF)
    share = half // NX

    def h_copy(e):
        return pltpu.make_async_remote_copy(
            src_ref=quarter_send.at[pl.ds(pl.multiple_of(lax.rem(x + e, NX) * share, share), share)],
            dst_ref=quarter_recv.at[pl.ds((e - 1) * share, share)],
            send_sem=h_send.at[e - 1], recv_sem=h_recv.at[e - 1],
            device_id=at_dir(e, 0), device_id_type=MESH,
        )

    for e in range(1, NX):
        h_copy(e).start()
    total = quarter_own[pl.ds(pl.multiple_of(x * share, share), share), :]
    for e in range(1, NX):
        h_copy(e).wait()
    for e in range(1, NX):
        total = total + quarter_recv[(e - 1) * share : e * share, :].astype(F32)

    def place(ex, ec):
        at = lax.rem(core + ec, 2) * half + lax.rem(x + NX - ex, NX) * share
        return pl.ds(pl.multiple_of(at, share), share)

    grad_all[place(0, 0), :] = total.astype(BF)

    def k_copy(n, came=False):
        ex, ec = group[n]
        rows = place(ex, ec) if came else place(0, 0)
        return pltpu.make_async_remote_copy(
            src_ref=grad_all.at[rows], dst_ref=grad_all.at[rows],
            send_sem=k_send.at[n], recv_sem=k_recv.at[n],
            device_id=at_dir(ex, ec), device_id_type=MESH,
        )

    for n in range(len(group)):
        k_copy(n).start()
    for n in range(len(group)):
        k_copy(n, came=True).wait_recv()
    grad_v_ref[...] = grad_all[0:half, :].astype(F32).T
    grad_p_ref[...] = grad_all[half : 2 * half, :].astype(F32).T

    for n in range(len(group)):
        k_copy(n).wait_send()

    def drain(q, carry):
        for e in range(1, NY):
            a_copy(q, e).wait_send()
            e_copy(q, e).wait_send()
        for e in range(1, NZ):
            b_copy(q, e).wait_send()
            d_copy(q, e).wait_send()
        return carry

    lax.fori_loop(0, TILES, drain, 0)


def shards(direction_angles, positions, normal_angles, areas, pressure, velocity, targets):
    cases = targets.shape[1]
    patches = positions.shape[1]
    dirs = direction_angles.shape[1]
    total_patches = patches * lax.axis_size("surf")
    owners = NY * NZ
    angles = direction_angles.reshape(2, owners, TILES, OWN).transpose(0, 2, 1, 3).reshape(2, dirs)
    vmem = pl.BlockSpec(memory_space=pltpu.VMEM)
    half = 2 * cases
    dma = pltpu.SemaphoreType.DMA
    slots = 2 * TILES + 1
    return pl.pallas_call(
        functools.partial(body, total_patches),
        out_shape=(
            jax.ShapeDtypeStruct((dirs // owners, half), F32),
            jax.ShapeDtypeStruct((patches, half), F32),
            jax.ShapeDtypeStruct((patches, half), F32),
        ),
        in_specs=[vmem] * 6 + [pl.BlockSpec(memory_space=pl.ANY)],
        out_specs=(vmem, vmem, vmem),
        scratch_shapes=[
            pltpu.VMEM((TILES * OWN, cases), F32),
            pltpu.VMEM((32, dirs), F32),
            pltpu.VMEM((32, patches), F32),
            pltpu.VMEM((8, dirs), F32),
            pltpu.VMEM((dirs, 8), F32),
            pltpu.VMEM((dirs, 32), BF),
            pltpu.VMEM((32, patches), BF),
            pltpu.VMEM((8, patches), F32),
            pltpu.VMEM((2 * patches, 4 * half), BF),
            pltpu.VMEM((slots * SUB, patches), BF),
            pltpu.VMEM((slots * SUB, patches), BF),
            pltpu.VMEM((slots * SUB, patches), BF),
            pltpu.VMEM((slots * SUB, patches), BF),
            pltpu.VMEM((TILES * (NY - 1) * SUB, half), BF),
            pltpu.VMEM((TILES * SUB, half), F32),
            pltpu.VMEM((TILES * (NY - 1) * SUB, half), BF),
            pltpu.VMEM((TILES * SUB, half), F32),
            pltpu.VMEM((TILES * SUB, half), BF),
            pltpu.VMEM((TILES * (NZ - 1) * OWN, half), BF),
            pltpu.VMEM((TILES * ROWS, half), BF),
            pltpu.VMEM((4 * half, patches), F32),
            pltpu.VMEM((half, patches), BF),
            pltpu.VMEM((half, patches), BF),
            pltpu.VMEM((half, patches), F32),
            pltpu.VMEM((half, patches), BF),
            pltpu.VMEM((half // NX * (NX - 1), patches), BF),
            pltpu.VMEM((2 * half, patches), BF),
            dma,
            dma((TILES * (NY - 1),)), dma((TILES * (NY - 1),)),
            dma((TILES * (NZ - 1),)), dma((TILES * (NZ - 1),)),
            dma((TILES * (NZ - 1),)), dma((TILES * (NZ - 1),)),
            dma((TILES * (NY - 1),)), dma((TILES * (NY - 1),)),
            dma, dma,
            dma((NX - 1,)), dma((NX - 1,)),
            dma((2 * NX - 1,)), dma((2 * NX - 1,)),
        ],
        compiler_params=pltpu.CompilerParams(
            collective_id=0, has_side_effects=True, vmem_limit_bytes=56 * 2**20
        ),
    )(
        angles, positions, normal_angles, areas.reshape(1, patches), pressure, velocity, targets
    )


def solution(mesh):
    in_specs = (
        P(None, "dir"),
        P(None, "surf"),
        P(None, "surf"),
        P("surf"),
        P("surf", None),
        P("surf", None),
        P("dir", None),
    )
    out_specs = (P(("dir", "surf"), None), P("surf", None), P("surf", None))
    return jax.shard_map(shards, mesh=mesh, in_specs=in_specs, out_specs=out_specs, check_vma=False)
```

time: 449 us -> 83.1 us (0.19)
  waiting for transfers between devices: 219 us -> 0 us
  other arithmetic: 137 us -> 0 us
  Pallas kernels: 0 us -> 71 us
  matrix products: 32.2 us -> 0 us
  local copies, waits for them, and re-layouts: 35.4 us -> 11.1 us
  between operations: 14.1 us -> 0.66 us
  loops' own time: 8.22 us -> 0 us
    psum x2 -> x0, waiting for transfers between devices: 219 us -> none  [the longest x1 154 us: shards(): totals = lax.psum(forward, 'surf')]
    convert_element_type x13 -> x0, other arithmetic: 121 us -> none  [the longest x12 120 us: kernel_tile(): cosine.astype(jnp.bfloat16)]
    pallas_call x0 -> x1, Pallas kernels: none -> 71 us  [shards(): pl.pallas_call(functools.partial(body, total_patches), out_shape=(jax.Sha...]
    dot_general x12 -> x0, matrix products: 32.2 us -> none  [the longest x6 27.3 us: forward_step(): jnp.dot(kernel, stacked, preferred_element_type=jnp.float32)]
    dynamic_slice x30 -> x0, local copies, waits for them, and re-layouts: 23.1 us -> none  [the longest x12 11.1 us: shards(): lax.scan(forward_step, initial, jnp.arange(patch_count // block_rows, dty...]
    neg x12 -> x0, other arithmetic: 8.91 us -> none  [the longest x6 4.58 us: combine_terms(): -column * dip_real]
    another operation x2 -> x0, loops' own time: 8.22 us -> none  [the longest x1 4.25 us: shards(): lax.map(one_block, jnp.arange(patch_count // rows_each, dtype=jnp.int32))]
    unnamed x9 -> x4, local copies, waits for them, and re-layouts: 0.75 us -> 8.19 us
  transfers between devices with their start and end apart: 2 -> 0, of which waited for: 2 -> 0; matrix products, arithmetic and copies ran while one was open for 0% -> 0% of each run, Pallas kernels for 0% -> 0%
where the time goes in v1:
time: 83.1 us; the launch traced here: 82.7 us
  Pallas kernels  71 us (85%)
  local copies, waits for them, and re-layouts  11.1 us (13%)
    pallas_call x1, Pallas kernels, shards(): pl.pallas_call(functools.partial(body, total_patches), out_shape=(jax.Sha...  71 us
    unnamed x4, local copies, waits for them, and re-layouts  8.19 us

profile of v1, /device:TPU:1, one launch (start us, length us, event | category | flops | bytes accessed | tf_op | source)
XLA Modules:
  0.0 82.7 jit_solution(13402685401476276759)
XLA Ops:
  0.6 1.3 %reshape.17.areas_ref = f32[1,768]{1,0:T(1,128)} reshape(f32[768]{0:T(1024)} %param.10) | data formatting | bytes 6144 | tf_op jit(solution)/shard_map/reshape | solution.py:443
  1.9 0.9 %reshape.15 = f32[2,32,4,32]{3,2,1,0:T(4,128)S(1)} reshape(f32[2,4096]{1,0:T(2,128)} %param.7) | data formatting | bytes 65536 | tf_op jit(solution)/shard_map/reshape | solution.py:388
  2.8 0.7 reshape.16.angles_ref
  3.5 3.2 %copy.11.targets_hbm = f32[4096,64]{1,0:T(8,128)} copy(f32[4096,64]{0,1:T(8,128)} %param.13) | data formatting | bytes 2097152 | tf_op args[6]
  6.7 71.0 %shard_map.94 = (f32[128,128]{1,0:T(8,128)}, f32[768,128]{1,0:T(8,128)}, f32[768,128]{1,0:T(8,128)}) custom-call(f32[2,4096]{1,0:T(2,128)} %reshape.16.angles_ref, f32[3,768]{1,0:T(4,128)} %positions_ref.1, f32[2,768]{1,0:T(2,128)} %normals_ref.1, f32[1,768]{1,0:T(1,128)} %reshape.17.areas_ref, bf16[768,128]{1,0:T(8,128)(2,1)} %pressure_ref.1, ...), custom_call_target="tpu_custom_call" | custom-call | tf_op jit(solution)/shard_map/pallas_call | solution.py:393
  77.7 1.5 %copy.17 = f32[128,128]{1,0:T(8,128)} copy(f32[128,128]{1,0:T(8,128)} %get-tuple-element.6) | data formatting | bytes 131072
  79.2 1.8 %copy.18 = f32[768,128]{1,0:T(8,128)} copy(f32[768,128]{1,0:T(8,128)} %get-tuple-element.7) | data formatting | bytes 786432
  81.0 1.8 %copy.19 = f32[768,128]{1,0:T(8,128)} copy(f32[768,128]{1,0:T(8,128)} %get-tuple-element.8) | data formatting | bytes 786432
  (1 shorter events, 0.0 us)

commit v2 on v1

--- a/solution.py
+++ b/solution.py
@@ -19,6 +19,7 @@
 SUB = NZ * OWN
 ROWS = NY * SUB
 DELTAS = (2, 1, 3, 0)
+OURS = 3
 SLOT_OF_SEND = {1: 2, 2: 0, 3: 1}
 
 ROOT2 = math.sqrt(2.0)
@@ -63,13 +64,14 @@
 def body(
     total_patches,
     angles_ref, positions_ref, normals_ref, areas_ref, pressure_ref, velocity_ref, targets_hbm,
-    responses_ref, grad_p_ref, grad_v_ref,
-    targets_ref, split_t, split_x, t_rows, t_cols, t_lhs, x_rhs, face_rows, weights,
+    responses_ref, grads_ref,
+    targets_t, targets_ref, angle_rows, angle_cols, angle_perm, split_t, split_x, t_rows, t_cols, t_lhs, x_rhs, face_rows, weights,
     cos_a, sin_a, cos_b, sin_b,
-    part_send, part_own, part_recv, row_own, row_send, row_recv, res_all, acc,
+    part_send, part_recv, part_own, row_own, row_send, row_recv, res_all, acc,
     half_send, half_recv, quarter_own, quarter_send, quarter_recv, grad_all,
-    local_sem, a_send, a_recv, b_send, b_recv, d_send, d_recv, e_send, e_recv,
-    g_send, g_recv, h_send, h_recv, k_send, k_recv,
+    local_sem, a_send, a_recv, b_send, b_recv, d_send, d_recv,
+    e_send, e_recv,
+    g_send, g_recv, h_send, h_recv, k_send, k_recv, m_send, m_recv,
 ):
     dir_index = lax.axis_index("dir")
     surf_index = lax.axis_index("surf")
@@ -86,7 +88,7 @@
     def at_dir(ex, ec):
         return (lax.rem(x + ex, NX) * 2 + lax.rem(core + ec, 2), surf_index)
 
-    group = [(ex, ec) for ex in range(NX) for ec in range(2) if ex or ec]
+    group = [(ex, 0) for ex in range(1, NX)] + [(0, 1)]
     barrier = pltpu.get_barrier_semaphore()
     for e in range(1, NY):
         pl.semaphore_signal(barrier, inc=1, device_id=at_y(e), device_id_type=MESH)
@@ -97,12 +99,19 @@
 
     own_rows = TILES * OWN
     fetch = pltpu.make_async_copy(
-        targets_hbm.at[pl.ds(pl.multiple_of(surf_index * own_rows, own_rows), own_rows)],
-        targets_ref, local_sem,
+        targets_hbm.at[:, pl.ds(pl.multiple_of(surf_index * own_rows, own_rows), own_rows)],
+        targets_t, local_sem,
     )
     fetch.start()
 
-    tx, ty, tz = unit_rows(angles_ref[...])
+    angle_rows[...] = jnp.zeros_like(angle_rows)
+    angle_rows[0:2, :] = angles_ref[...]
+    angle_cols[...] = angle_rows[...].T
+    for q in range(TILES):
+        for owner in range(NY * NZ):
+            begin, source = q * ROWS + owner * OWN, owner * own_rows + q * OWN
+            angle_perm[begin : begin + OWN, :] = angle_cols[source : source + OWN, :]
+    tx, ty, tz = unit_rows(angle_perm[...].T)
     split_t[...] = jnp.zeros_like(split_t)
     split_x[...] = jnp.zeros_like(split_x)
     t_rows[...] = jnp.zeros_like(t_rows)
@@ -119,7 +128,9 @@
     t_cols[...] = t_rows[...].T
 
     face_rows[...] = jnp.zeros_like(face_rows)
-    scale_row = areas_ref[...] * F32(1.0 / math.sqrt(total_patches))
+    for at in range(areas_ref.shape[0]):
+        face_rows[3:4, 128 * at : 128 * (at + 1)] = areas_ref[at : at + 1, :]
+    scale_row = face_rows[3:4, :] * F32(1.0 / math.sqrt(total_patches))
     for k, row in enumerate(unit_rows(normals_ref[...])):
         face_rows[k : k + 1, :] = row
     face_rows[3:4, :] = scale_row
@@ -150,21 +161,26 @@
 
     quarter = SUB // 4
 
-    def forward_step(tq, tj, tslot, mq, mj, mslot):
-        tc, ts = (cos_a, sin_a) if tj % 2 == 0 else (cos_b, sin_b)
-        mc, ms = (cos_a, sin_a) if mj % 2 == 0 else (cos_b, sin_b)
-        rows = pl.ds(pl.multiple_of(mslot * SUB, SUB), SUB)
+    def forward_step(q, j, after=None):
+        def make(piece):
+            if after is not None:
+                tq, tj, slot = after
+                tc, ts = (cos_a, sin_a) if tj % 2 == 0 else (cos_b, sin_b)
+                trig_piece(tq, tj, tc, ts, slot, piece * quarter, quarter)
+
+        mc, ms = (cos_a, sin_a) if j % 2 == 0 else (cos_b, sin_b)
+        rows = pl.ds(pl.multiple_of((2 * q + j // 2) * SUB, SUB), SUB)
         halves = []
         for h in range(2):
             columns = slice(4 * cases * h, 4 * cases * (h + 1))
             g = jnp.dot(mc[rows, :], weights[0:patches, columns], preferred_element_type=F32)
-            trig_piece(tq, tj, tc, ts, tslot, 2 * h * quarter, quarter)
+            make(2 * h)
             g = g + jnp.dot(
                 ms[rows, :], weights[patches : 2 * patches, columns], preferred_element_type=F32
             )
-            trig_piece(tq, tj, tc, ts, tslot, (2 * h + 1) * quarter, quarter)
+            make(2 * h + 1)
             halves.append(g)
-        t_at = t_cols[pl.ds(sub_row(mq, mj), SUB), :]
+        t_at = t_cols[pl.ds(sub_row(q, j), SUB), :]
         lo, hi = halves
         return (
             lo[:, : 2 * cases]
@@ -173,10 +189,12 @@
             + t_at[:, 2:3] * hi[:, 2 * cases :]
         )
 
+    def a_rows(q, e):
+        return pl.ds(pl.multiple_of((q * (NY - 1) + e - 1) * SUB, SUB), SUB)
+
     def a_copy(q, e):
-        at = pl.multiple_of((q * (NY - 1) + e - 1) * SUB, SUB)
-        return pltpu.make_async_remote_copy(
-            src_ref=part_send.at[pl.ds(at, SUB)], dst_ref=part_recv.at[pl.ds(at, SUB)],
+        return pltpu.make_async_remote_copy(
+            src_ref=part_send.at[a_rows(q, e)], dst_ref=part_recv.at[a_rows(q, e)],
             send_sem=a_send.at[q * (NY - 1) + e - 1], recv_sem=a_recv.at[q * (NY - 1) + e - 1],
             device_id=at_y(e), device_id_type=MESH,
         )
@@ -191,7 +209,7 @@
 
     def d_copy(q, e, came=False):
         source = lax.rem(z + NZ - e, NZ) if came else z
-        rows = pl.ds(pl.multiple_of(q * ROWS + 3 * SUB + source * OWN, OWN), OWN)
+        rows = pl.ds(pl.multiple_of(q * ROWS + OURS * SUB + source * OWN, OWN), OWN)
         return pltpu.make_async_remote_copy(
             src_ref=res_all.at[rows], dst_ref=res_all.at[rows],
             send_sem=d_send.at[q * (NZ - 1) + e - 1], recv_sem=d_recv.at[q * (NZ - 1) + e - 1],
@@ -200,25 +218,39 @@
 
     def e_copy(q, e):
         return pltpu.make_async_remote_copy(
-            src_ref=res_all.at[pl.ds(pl.multiple_of(q * ROWS + 3 * SUB, SUB), SUB)],
+            src_ref=res_all.at[pl.ds(pl.multiple_of(q * ROWS + OURS * SUB, SUB), SUB)],
             dst_ref=res_all.at[pl.ds(pl.multiple_of(q * ROWS + SLOT_OF_SEND[e] * SUB, SUB), SUB)],
             send_sem=e_send.at[q * (NY - 1) + e - 1], recv_sem=e_recv.at[q * (NY - 1) + e - 1],
             device_id=at_y(e), device_id_type=MESH,
         )
 
-    def send_part(q, j, partial):
-        e = DELTAS[j]
-        at = pl.multiple_of((q * (NY - 1) + e - 1) * SUB, SUB)
-        part_send[pl.ds(at, SUB), :] = partial.astype(BF)
-        a_copy(q, e).start()
-
-    def forward_tile(q):
-        send_part(q, 0, forward_step(q, 1, 2 * q, q, 0, 2 * q))
-        send_part(q, 1, forward_step(q, 2, 2 * q + 1, q, 1, 2 * q))
-        send_part(q, 2, forward_step(q, 3, 2 * q + 1, q, 2, 2 * q + 1))
-        after = lax.rem(q + 1, TILES)
-        own = forward_step(after, 0, 2 * q + 2, q, 3, 2 * q + 1)
-        part_own[pl.ds(pl.multiple_of(q * SUB, SUB), SUB), :] = own
+    def step_0(q):
+        part_send[a_rows(q, DELTAS[0]), :] = forward_step(q, 0, (q, 1, 2 * q)).astype(BF)
+
+    def step_1(q):
+        part_send[a_rows(q, DELTAS[1]), :] = forward_step(q, 1, (q, 2, 2 * q + 1)).astype(BF)
+
+        @pl.when(q == 0)
+        def _():
+            pl.semaphore_wait(barrier, (NY - 1) + (NZ - 1) + len(group))
+
+        a_copy(q, DELTAS[0]).start()
+        a_copy(q, DELTAS[1]).start()
+
+    def step_2(q):
+        part_send[a_rows(q, DELTAS[2]), :] = forward_step(q, 2, (q, 3, 2 * q + 1)).astype(BF)
+        a_copy(q, DELTAS[2]).start()
+
+    def step_3(q):
+        rows = pl.ds(pl.multiple_of(q * SUB, SUB), SUB)
+
+        @pl.when(q < TILES - 1)
+        def _():
+            part_own[rows, :] = forward_step(q, 3, (q + 1, 0, 2 * q + 2))
+
+        @pl.when(q == TILES - 1)
+        def _():
+            part_own[rows, :] = forward_step(q, 3)
 
     def sum_over_y(q):
         rows = pl.ds(pl.multiple_of(q * SUB, SUB), SUB)
@@ -226,8 +258,7 @@
         for e in range(1, NY):
             a_copy(q, e).wait_recv()
         for e in range(1, NY):
-            at = pl.multiple_of((q * (NY - 1) + e - 1) * SUB, SUB)
-            total = total + part_recv[pl.ds(at, SUB), :].astype(F32)
+            total = total + part_recv[a_rows(q, e), :].astype(F32)
         row_own[rows, :] = total
         row_send[rows, :] = total.astype(BF)
         for e in range(1, NZ):
@@ -246,7 +277,7 @@
         magnitude = jnp.sqrt(real * real + imag * imag)
         weight = (magnitude - targets_ref[out_rows, :]) / jnp.maximum(magnitude, FLOOR)
         residual = jnp.concatenate([weight * real, weight * imag], axis=1).astype(BF)
-        res_all[pl.ds(pl.multiple_of(q * ROWS + 3 * SUB + z * OWN, OWN), OWN), :] = residual
+        res_all[pl.ds(pl.multiple_of(q * ROWS + OURS * SUB + z * OWN, OWN), OWN), :] = residual
         for e in range(1, NZ):
             d_copy(q, e).start()
 
@@ -259,7 +290,7 @@
     def adjoint_tile(q):
         for e in range(1, NY):
             e_copy(q, e).wait_recv()
-        for parity, (cos_ref, sin_ref) in enumerate(((cos_a, sin_a), (cos_b, sin_b))):
+        for parity, cos_ref, sin_ref in ((1, cos_b, sin_b), (0, cos_a, sin_a)):
             pieces, t_pieces = [], []
             for j in (parity, parity + 2):
                 at = pl.multiple_of(q * ROWS + j * SUB, SUB)
@@ -282,17 +313,24 @@
     for begin in range(0, SUB, quarter):
         trig_piece(0, 0, cos_a, sin_a, 0, begin, quarter)
     fetch.wait()
-    pl.semaphore_wait(barrier, (NY - 1) + (NZ - 1) + len(group))
+    targets_ref[...] = targets_t[...].T
 
     def step(it, carry):
-        pl.when(it < TILES)(lambda: forward_tile(it))
-        pl.when(it >= 4)(lambda: adjoint_tile(it - 4))
-        pl.when(jnp.logical_and(it >= 3, it < TILES + 3))(lambda: share_over_y(it - 3))
-        pl.when(jnp.logical_and(it >= 2, it < TILES + 2))(lambda: make_residual(it - 2))
-        pl.when(jnp.logical_and(it >= 1, it < TILES + 1))(lambda: sum_over_y(it - 1))
+        def when(work, lag):
+            inside = jnp.logical_and(it >= lag, it < TILES + lag)
+            pl.when(inside)(lambda: work(it - lag))
+
+        when(step_0, 0)
+        when(step_1, 0)
+        when(make_residual, 3)
+        when(step_2, 0)
+        when(step_3, 0)
+        when(share_over_y, 4)
+        when(sum_over_y, 1)
+        when(adjoint_tile, 6)
         return carry
 
-    lax.fori_loop(0, TILES + 4, step, 0)
+    lax.fori_loop(0, TILES + 6, step, 0)
 
     half = 2 * cases
 
@@ -348,24 +386,36 @@
 
     grad_all[place(0, 0), :] = total.astype(BF)
 
-    def k_copy(n, came=False):
-        ex, ec = group[n]
-        rows = place(ex, ec) if came else place(0, 0)
+    def k_copy(e, came=False):
+        rows = place(e, 0) if came else place(0, 0)
         return pltpu.make_async_remote_copy(
             src_ref=grad_all.at[rows], dst_ref=grad_all.at[rows],
-            send_sem=k_send.at[n], recv_sem=k_recv.at[n],
-            device_id=at_dir(ex, ec), device_id_type=MESH,
-        )
-
-    for n in range(len(group)):
-        k_copy(n).start()
-    for n in range(len(group)):
-        k_copy(n, came=True).wait_recv()
-    grad_v_ref[...] = grad_all[0:half, :].astype(F32).T
-    grad_p_ref[...] = grad_all[half : 2 * half, :].astype(F32).T
-
-    for n in range(len(group)):
-        k_copy(n).wait_send()
+            send_sem=k_send.at[e - 1], recv_sem=k_recv.at[e - 1],
+            device_id=at_dir(e, 0), device_id_type=MESH,
+        )
+
+    def m_copy(e, came=False):
+        rows = place(e, 1) if came else place(e, 0)
+        return pltpu.make_async_remote_copy(
+            src_ref=grad_all.at[rows], dst_ref=grad_all.at[rows],
+            send_sem=m_send.at[e], recv_sem=m_recv.at[e],
+            device_id=at_dir(0, 1), device_id_type=MESH,
+        )
+
+    for e in range(1, NX):
+        k_copy(e).start()
+    m_copy(0).start()
+    for e in (1, 3, 2):
+        k_copy(e, came=True).wait_recv()
+        m_copy(e).start()
+    for e in range(NX):
+        m_copy(e, came=True).wait_recv()
+    grads_ref[...] = grad_all[...]
+
+    for e in range(1, NX):
+        k_copy(e).wait_send()
+    for e in range(NX):
+        m_copy(e).wait_send()
 
     def drain(q, carry):
         for e in range(1, NY):
@@ -379,28 +429,37 @@
     lax.fori_loop(0, TILES, drain, 0)
 
 
+def finish(responses_ref, grads_ref, out_ref, grad_p_ref, grad_v_ref):
+    half = grads_ref.shape[0] // 2
+    out_ref[...] = responses_ref[...]
+    grad_v_ref[...] = grads_ref[0:half, :].astype(F32).T
+    grad_p_ref[...] = grads_ref[half : 2 * half, :].astype(F32).T
+
+
 def shards(direction_angles, positions, normal_angles, areas, pressure, velocity, targets):
     cases = targets.shape[1]
     patches = positions.shape[1]
     dirs = direction_angles.shape[1]
     total_patches = patches * lax.axis_size("surf")
     owners = NY * NZ
-    angles = direction_angles.reshape(2, owners, TILES, OWN).transpose(0, 2, 1, 3).reshape(2, dirs)
     vmem = pl.BlockSpec(memory_space=pltpu.VMEM)
     half = 2 * cases
     dma = pltpu.SemaphoreType.DMA
-    slots = 2 * TILES + 1
-    return pl.pallas_call(
+    slots = 2 * TILES
+    responses, grads = pl.pallas_call(
         functools.partial(body, total_patches),
         out_shape=(
             jax.ShapeDtypeStruct((dirs // owners, half), F32),
-            jax.ShapeDtypeStruct((patches, half), F32),
-            jax.ShapeDtypeStruct((patches, half), F32),
+            jax.ShapeDtypeStruct((2 * half, patches), BF),
         ),
         in_specs=[vmem] * 6 + [pl.BlockSpec(memory_space=pl.ANY)],
-        out_specs=(vmem, vmem, vmem),
+        out_specs=(vmem, vmem),
         scratch_shapes=[
+            pltpu.VMEM((cases, TILES * OWN), F32),
             pltpu.VMEM((TILES * OWN, cases), F32),
+            pltpu.VMEM((8, dirs), F32),
+            pltpu.VMEM((dirs, 8), F32),
+            pltpu.VMEM((dirs, 8), F32),
             pltpu.VMEM((32, dirs), F32),
             pltpu.VMEM((32, patches), F32),
             pltpu.VMEM((8, dirs), F32),
@@ -414,8 +473,8 @@
             pltpu.VMEM((slots * SUB, patches), BF),
             pltpu.VMEM((slots * SUB, patches), BF),
             pltpu.VMEM((TILES * (NY - 1) * SUB, half), BF),
+            pltpu.VMEM((TILES * (NY - 1) * SUB, half), BF),
             pltpu.VMEM((TILES * SUB, half), F32),
-            pltpu.VMEM((TILES * (NY - 1) * SUB, half), BF),
             pltpu.VMEM((TILES * SUB, half), F32),
             pltpu.VMEM((TILES * SUB, half), BF),
             pltpu.VMEM((TILES * (NZ - 1) * OWN, half), BF),
@@ -434,14 +493,26 @@
             dma((TILES * (NY - 1),)), dma((TILES * (NY - 1),)),
             dma, dma,
             dma((NX - 1,)), dma((NX - 1,)),
-            dma((2 * NX - 1,)), dma((2 * NX - 1,)),
+            dma((NX - 1,)), dma((NX - 1,)),
+            dma((NX,)), dma((NX,)),
         ],
         compiler_params=pltpu.CompilerParams(
             collective_id=0, has_side_effects=True, vmem_limit_bytes=56 * 2**20
         ),
     )(
-        angles, positions, normal_angles, areas.reshape(1, patches), pressure, velocity, targets
+        direction_angles, positions, normal_angles, areas.reshape(patches // 128, 128),
+        pressure, velocity, targets.T,
     )
+    return pl.pallas_call(
+        finish,
+        out_shape=(
+            jax.ShapeDtypeStruct((dirs // owners, half), F32),
+            jax.ShapeDtypeStruct((patches, half), F32),
+            jax.ShapeDtypeStruct((patches, half), F32),
+        ),
+        in_specs=[vmem] * 2,
+        out_specs=(vmem, vmem, vmem),
+    )(responses, grads)
 
 
 def solution(mesh):

time: 83.1 us -> 66.1 us (0.80)
  local copies, waits for them, and re-layouts: 11.1 us -> 0 us
  Pallas kernels: 71 us -> 65.3 us
    unnamed x4 -> x0, local copies, waits for them, and re-layouts: 8.19 us -> none
    pallas_call x1, Pallas kernels: 71 us -> 63.2 us  [shards(): pl.pallas_call(functools.partial(body, total_patches), out_shape=(jax.Sha...]
    reshape x4 -> x0, local copies, waits for them, and re-layouts: 2.89 us -> none  [the longest x3 1.63 us: shards(): direction_angles.reshape(2, owners, TILES, OWN).transpose(0, 2, 1, 3)]
    pallas_call x0 -> x1, Pallas kernels: none -> 2.08 us  [shards(): pl.pallas_call(finish, out_shape=(jax.ShapeDtypeStruct((dirs // owners, h...]
where the time goes in v2:
time: 66.1 us; the launch traced here: 66 us
  Pallas kernels  65.3 us (99%)
    pallas_call x1, Pallas kernels, shards(): pl.pallas_call(functools.partial(body, total_patches), out_shape=(jax.Sha...  63.2 us
    pallas_call x1, Pallas kernels, shards(): pl.pallas_call(finish, out_shape=(jax.ShapeDtypeStruct((dirs // owners, h...  2.08 us

profile of v2, /device:TPU:1, one launch (start us, length us, event | category | flops | bytes accessed | tf_op | source)
XLA Modules:
  0.0 66.0 jit_solution(5180791143286144471)
XLA Ops:
  0.6 63.2 %shard_map.94 = (f32[128,128]{1,0:T(8,128)}, bf16[256,768]{1,0:T(8,128)(2,1)}) custom-call(f32[2,4096]{1,0:T(2,128)} %angles_ref.1, f32[3,768]{1,0:T(4,128)} %positions_ref.1, f32[2,768]{1,0:T(2,128)} %normals_ref.1, f32[6,128]{1,0:T(8,128)} %bitcast.3, bf16[768,128]{1,0:T(8,128)(2,1)} %pressure_ref.1, bf16[768,128]{1,0:T(8,128)(2,1)} %velocity_ref.1, ...), custom_call_target="tpu_custom_call" | custom-call | tf_op jit(solution)/shard_map/pallas_call | solution.py:449
  63.9 2.1 %shard_map.95 = (f32[128,128]{1,0:T(8,128)}, f32[768,128]{1,0:T(8,128)}, f32[768,128]{1,0:T(8,128)}) custom-call(f32[128,128]{1,0:T(8,128)} %get-tuple-element.5.responses_ref, bf16[256,768]{1,0:T(8,128)(2,1)} %get-tuple-element.6.grads_ref), custom_call_target="tpu_custom_call" | custom-call | tf_op jit(solution)/shard_map/pallas_call | solution.py:506

commit v3 on v2

--- a/solution.py
+++ b/solution.py
@@ -24,7 +24,6 @@
 
 ROOT2 = math.sqrt(2.0)
 SIN_HALF = [c * ROOT2 for c in (3.14158198, -5.1671413, 2.54188707, -0.55460885)]
-COS_HALF = [c * ROOT2 for c in (0.99999325, -4.93393467, 4.0412481, -1.22203176)]
 SIN_FINE = [c * ROOT2 for c in (3.14159258, -5.16770687, 2.55003119, -0.59804419, 0.07721839)]
 COS_FINE = [c * ROOT2 for c in (0.99999995, -4.93479283, 4.05841135, -1.33187657, 0.21968961)]
 
@@ -36,16 +35,20 @@
     return value
 
 
-def cos_sin(cycles, sin_half, cos_half):
+def cos_sin(cycles):
+    rest = cycles - jnp.round(cycles)
+    half_sine = horner(SIN_HALF, rest * rest) * rest
+    double = half_sine * half_sine
+    left = jnp.maximum(2.0 - double, 1e-20)
+    return 1.0 - double, half_sine * (left * lax.rsqrt(left))
+
+
+def fine_cos_sin(angle):
+    cycles = angle * F32(1.0 / (2.0 * math.pi))
     rest = cycles - jnp.round(cycles)
     square = rest * rest
-    half_sine = horner(sin_half, square) * rest
-    half_cosine = horner(cos_half, square)
-    return 1.0 - half_sine * half_sine, half_sine * half_cosine
-
-
-def fine_cos_sin(angle):
-    return cos_sin(angle * F32(1.0 / (2.0 * math.pi)), SIN_FINE, COS_FINE)
+    half_sine = horner(SIN_FINE, square) * rest
+    return 1.0 - half_sine * half_sine, half_sine * horner(COS_FINE, square)
 
 
 def unit_rows(angles):
@@ -154,7 +157,7 @@
         angle = jnp.dot(
             t_lhs[pl.ds(sub_row(q, j) + begin, count), :], x_rhs[...], preferred_element_type=F32
         )
-        cosine, sine = cos_sin(angle, SIN_HALF, COS_HALF)
+        cosine, sine = cos_sin(angle)
         at = pl.multiple_of(slot * SUB + begin, count)
         cos_ref[pl.ds(at, count), :] = cosine.astype(BF)
         sin_ref[pl.ds(at, count), :] = sine.astype(BF)
@@ -287,28 +290,36 @@
         for e in range(1, NY):
             e_copy(q, e).start()
 
+    def adjoint_sides(q, parity):
+        pieces, t_pieces = [], []
+        for j in (parity, parity + 2):
+            at = pl.multiple_of(q * ROWS + j * SUB, SUB)
+            pieces.append(res_all[pl.ds(at, SUB), :].astype(F32))
+            t_pieces.append(t_rows[:, pl.ds(sub_row(q, j), SUB)])
+        turned = jnp.concatenate(pieces, axis=0).T
+        t_at = jnp.concatenate(t_pieces, axis=1)
+        swapped = jnp.concatenate([turned[cases:], -turned[:cases]], axis=0)
+        with_cos, with_sin = [swapped.astype(BF)], [turned.astype(BF)]
+        for k in range(3):
+            with_cos.append((swapped * t_at[k : k + 1, :]).astype(BF))
+            with_sin.append((turned * t_at[k : k + 1, :]).astype(BF))
+        return jnp.concatenate(with_cos, axis=0), jnp.concatenate(with_sin, axis=0)
+
+    def adjoint_add(q, parity, sides, columns):
+        cos_ref, sin_ref = ((cos_a, sin_a), (cos_b, sin_b))[parity]
+        rows = pl.ds(pl.multiple_of(q * 2 * SUB, 2 * SUB), 2 * SUB)
+        acc[:, columns] += jnp.dot(
+            sides[0], cos_ref[rows, columns], preferred_element_type=F32
+        ) + jnp.dot(sides[1], sin_ref[rows, columns], preferred_element_type=F32)
+
+    first_sends = [e for e in SLOT_OF_SEND if SLOT_OF_SEND[e] % 2 == 1]
+    other_sends = [e for e in SLOT_OF_SEND if SLOT_OF_SEND[e] % 2 == 0]
+
     def adjoint_tile(q):
-        for e in range(1, NY):
-            e_copy(q, e).wait_recv()
-        for parity, cos_ref, sin_ref in ((1, cos_b, sin_b), (0, cos_a, sin_a)):
-            pieces, t_pieces = [], []
-            for j in (parity, parity + 2):
-                at = pl.multiple_of(q * ROWS + j * SUB, SUB)
-                pieces.append(res_all[pl.ds(at, SUB), :].astype(F32))
-                t_pieces.append(t_rows[:, pl.ds(sub_row(q, j), SUB)])
-            turned = jnp.concatenate(pieces, axis=0).T
-            t_at = jnp.concatenate(t_pieces, axis=1)
-            swapped = jnp.concatenate([turned[cases:], -turned[:cases]], axis=0)
-            with_cos, with_sin = [swapped.astype(BF)], [turned.astype(BF)]
-            for k in range(3):
-                with_cos.append((swapped * t_at[k : k + 1, :]).astype(BF))
-                with_sin.append((turned * t_at[k : k + 1, :]).astype(BF))
-            rows = pl.ds(pl.multiple_of(q * 2 * SUB, 2 * SUB), 2 * SUB)
-            acc[...] += jnp.dot(
-                jnp.concatenate(with_cos, axis=0), cos_ref[rows, :], preferred_element_type=F32
-            ) + jnp.dot(
-                jnp.concatenate(with_sin, axis=0), sin_ref[rows, :], preferred_element_type=F32
-            )
+        for parity, sends in ((1, first_sends), (0, other_sends)):
+            for e in sends:
+                e_copy(q, e).wait_recv()
+            adjoint_add(q, parity, adjoint_sides(q, parity), slice(0, patches))
 
     for begin in range(0, SUB, quarter):
         trig_piece(0, 0, cos_a, sin_a, 0, begin, quarter)
@@ -327,95 +338,114 @@
         when(step_3, 0)
         when(share_over_y, 4)
         when(sum_over_y, 1)
-        when(adjoint_tile, 6)
+        pl.when(it >= 6)(lambda: adjoint_tile(it - 6))
         return carry
 
-    lax.fori_loop(0, TILES + 6, step, 0)
+    lax.fori_loop(0, TILES + 5, step, 0)
 
     half = 2 * cases
-
-    def gradient(which):
+    share = half // NX
+    cuts = (slice(0, 512), slice(512, patches))
+    last = TILES - 1
+
+    def gradient(which, columns):
         if which == 0:
-            return acc[0:half, :] * scale_row
-        total = acc[half : 2 * half, :] * face_rows[0:1, :]
+            return acc[0:half, columns] * scale_row[:, columns]
+        total = acc[half : 2 * half, columns] * face_rows[0:1, columns]
         for k in range(1, 3):
-            total = total + acc[(k + 1) * half : (k + 2) * half, :] * face_rows[k : k + 1, :]
-        return total * scale_row
-
-    for which in range(2):
-        grad = gradient(which)
-
-        @pl.when(core == which)
-        def _():
-            quarter_own[...] = grad
-
-        @pl.when(core != which)
-        def _():
-            half_send[...] = grad.astype(BF)
-
-    g_copy = pltpu.make_async_remote_copy(
-        src_ref=half_send, dst_ref=half_recv, send_sem=g_send, recv_sem=g_recv,
-        device_id=at_dir(0, 1), device_id_type=MESH,
-    )
-    g_copy.start()
-    g_copy.wait()
-    chip = quarter_own[...] + half_recv[...].astype(F32)
-    quarter_own[...] = chip
-    quarter_send[...] = chip.astype(BF)
-    share = half // NX
-
-    def h_copy(e):
-        return pltpu.make_async_remote_copy(
-            src_ref=quarter_send.at[pl.ds(pl.multiple_of(lax.rem(x + e, NX) * share, share), share)],
-            dst_ref=quarter_recv.at[pl.ds((e - 1) * share, share)],
-            send_sem=h_send.at[e - 1], recv_sem=h_recv.at[e - 1],
+            begin = (k + 1) * half
+            total = total + acc[begin : begin + half, columns] * face_rows[k : k + 1, columns]
+        return total * scale_row[:, columns]
+
+    def g_copy(n):
+        return pltpu.make_async_remote_copy(
+            src_ref=half_send.at[:, cuts[n]], dst_ref=half_recv.at[:, cuts[n]],
+            send_sem=g_send.at[n], recv_sem=g_recv.at[n],
+            device_id=at_dir(0, 1), device_id_type=MESH,
+        )
+
+    def h_copy(n, e):
+        source = pl.ds(pl.multiple_of(lax.rem(x + e, NX) * share, share), share)
+        return pltpu.make_async_remote_copy(
+            src_ref=quarter_send.at[source, cuts[n]],
+            dst_ref=quarter_recv.at[pl.ds((e - 1) * share, share), cuts[n]],
+            send_sem=h_send.at[3 * n + e - 1], recv_sem=h_recv.at[3 * n + e - 1],
             device_id=at_dir(e, 0), device_id_type=MESH,
         )
-
-    for e in range(1, NX):
-        h_copy(e).start()
-    total = quarter_own[pl.ds(pl.multiple_of(x * share, share), share), :]
-    for e in range(1, NX):
-        h_copy(e).wait()
-    for e in range(1, NX):
-        total = total + quarter_recv[(e - 1) * share : e * share, :].astype(F32)
 
     def place(ex, ec):
         at = lax.rem(core + ec, 2) * half + lax.rem(x + NX - ex, NX) * share
         return pl.ds(pl.multiple_of(at, share), share)
 
-    grad_all[place(0, 0), :] = total.astype(BF)
-
-    def k_copy(e, came=False):
+    def k_copy(n, e, came=False):
         rows = place(e, 0) if came else place(0, 0)
         return pltpu.make_async_remote_copy(
-            src_ref=grad_all.at[rows], dst_ref=grad_all.at[rows],
-            send_sem=k_send.at[e - 1], recv_sem=k_recv.at[e - 1],
+            src_ref=grad_all.at[rows, cuts[n]], dst_ref=grad_all.at[rows, cuts[n]],
+            send_sem=k_send.at[3 * n + e - 1], recv_sem=k_recv.at[3 * n + e - 1],
             device_id=at_dir(e, 0), device_id_type=MESH,
         )
 
-    def m_copy(e, came=False):
+    def m_copy(n, e, came=False):
         rows = place(e, 1) if came else place(e, 0)
         return pltpu.make_async_remote_copy(
-            src_ref=grad_all.at[rows], dst_ref=grad_all.at[rows],
-            send_sem=m_send.at[e], recv_sem=m_recv.at[e],
+            src_ref=grad_all.at[rows, cuts[n]], dst_ref=grad_all.at[rows, cuts[n]],
+            send_sem=m_send.at[NX * n + e], recv_sem=m_recv.at[NX * n + e],
             device_id=at_dir(0, 1), device_id_type=MESH,
         )
 
-    for e in range(1, NX):
-        k_copy(e).start()
-    m_copy(0).start()
-    for e in (1, 3, 2):
-        k_copy(e, came=True).wait_recv()
-        m_copy(e).start()
-    for e in range(NX):
-        m_copy(e, came=True).wait_recv()
+    for e in first_sends:
+        e_copy(last, e).wait_recv()
+    adjoint_add(last, 1, adjoint_sides(last, 1), slice(0, patches))
+    for e in other_sends:
+        e_copy(last, e).wait_recv()
+    sides = adjoint_sides(last, 0)
+    for n, columns in enumerate(cuts):
+        adjoint_add(last, 0, sides, columns)
+        for which in range(2):
+            grad = gradient(which, columns)
+
+            @pl.when(core == which)
+            def _():
+                quarter_own[:, columns] = grad
+
+            @pl.when(core != which)
+            def _():
+                half_send[:, columns] = grad.astype(BF)
+
+        g_copy(n).start()
+    for n, columns in enumerate(cuts):
+        g_copy(n).wait_recv()
+        chip = quarter_own[:, columns] + half_recv[:, columns].astype(F32)
+        quarter_own[:, columns] = chip
+        quarter_send[:, columns] = chip.astype(BF)
+        for e in (2, 1, 3):
+            h_copy(n, e).start()
+    for n, columns in enumerate(cuts):
+        total = quarter_own[pl.ds(pl.multiple_of(x * share, share), share), columns]
+        for e in range(1, NX):
+            h_copy(n, e).wait_recv()
+        for e in range(1, NX):
+            total = total + quarter_recv[(e - 1) * share : e * share, columns].astype(F32)
+        grad_all[place(0, 0), columns] = total.astype(BF)
+        for e in (2, 1, 3):
+            k_copy(n, e).start()
+        m_copy(n, 0).start()
+    for n in range(2):
+        for e in (1, 3, 2):
+            k_copy(n, e, came=True).wait_recv()
+            m_copy(n, e).start()
+    for n in range(2):
+        for e in range(NX):
+            m_copy(n, e, came=True).wait_recv()
     grads_ref[...] = grad_all[...]
 
-    for e in range(1, NX):
-        k_copy(e).wait_send()
-    for e in range(NX):
-        m_copy(e).wait_send()
+    for n in range(2):
+        g_copy(n).wait_send()
+        for e in range(1, NX):
+            h_copy(n, e).wait_send()
+            k_copy(n, e).wait_send()
+        for e in range(NX):
+            m_copy(n, e).wait_send()
 
     def drain(q, carry):
         for e in range(1, NY):
@@ -491,10 +521,10 @@
             dma((TILES * (NZ - 1),)), dma((TILES * (NZ - 1),)),
             dma((TILES * (NZ - 1),)), dma((TILES * (NZ - 1),)),
             dma((TILES * (NY - 1),)), dma((TILES * (NY - 1),)),
-            dma, dma,
-            dma((NX - 1,)), dma((NX - 1,)),
-            dma((NX - 1,)), dma((NX - 1,)),
-            dma((NX,)), dma((NX,)),
+            dma((2,)), dma((2,)),
+            dma((2 * (NX - 1),)), dma((2 * (NX - 1),)),
+            dma((2 * (NX - 1),)), dma((2 * (NX - 1),)),
+            dma((2 * NX,)), dma((2 * NX,)),
         ],
         compiler_params=pltpu.CompilerParams(
             collective_id=0, has_side_effects=True, vmem_limit_bytes=56 * 2**20

time: 66.1 us -> 64.2 us (0.971)
  Pallas kernels: 65.3 us -> 63.4 us
    pallas_call x1, Pallas kernels: 63.2 us -> 61.3 us  [shards(): pl.pallas_call(functools.partial(body, total_patches), out_shape=(jax.Sha...]
where the time goes in v3:
time: 64.2 us; the launch traced here: 64.1 us
  Pallas kernels  63.4 us (99%)
    pallas_call x1, Pallas kernels, shards(): pl.pallas_call(functools.partial(body, total_patches), out_shape=(jax.Sha...  61.3 us
    pallas_call x1, Pallas kernels, shards(): pl.pallas_call(finish, out_shape=(jax.ShapeDtypeStruct((dirs // owners, h...  2.08 us

profile of v3, /device:TPU:1, one launch (start us, length us, event | category | flops | bytes accessed | tf_op | source)
XLA Modules:
  0.0 64.1 jit_solution(16584401557271899566)
XLA Ops:
  0.6 61.3 %shard_map.94 = (f32[128,128]{1,0:T(8,128)}, bf16[256,768]{1,0:T(8,128)(2,1)}) custom-call(f32[2,4096]{1,0:T(2,128)} %angles_ref.1, f32[3,768]{1,0:T(4,128)} %positions_ref.1, f32[2,768]{1,0:T(2,128)} %normals_ref.1, f32[6,128]{1,0:T(8,128)} %bitcast.3, bf16[768,128]{1,0:T(8,128)(2,1)} %pressure_ref.1, bf16[768,128]{1,0:T(8,128)(2,1)} %velocity_ref.1, ...), custom_call_target="tpu_custom_call" | custom-call | tf_op jit(solution)/shard_map/pallas_call | solution.py:479
  62.0 2.1 %shard_map.95 = (f32[128,128]{1,0:T(8,128)}, f32[768,128]{1,0:T(8,128)}, f32[768,128]{1,0:T(8,128)}) custom-call(f32[128,128]{1,0:T(8,128)} %get-tuple-element.5.responses_ref, bf16[256,768]{1,0:T(8,128)(2,1)} %get-tuple-element.6.grads_ref), custom_call_target="tpu_custom_call" | custom-call | tf_op jit(solution)/shard_map/pallas_call | solution.py:536

commit v4 on v3

--- a/solution.py
+++ b/solution.py
@@ -19,6 +19,7 @@
 SUB = NZ * OWN
 ROWS = NY * SUB
 DELTAS = (2, 1, 3, 0)
+FAR_FIRST = (4, 3, 5, 2, 6, 1, 7)
 OURS = 3
 SLOT_OF_SEND = {1: 2, 2: 0, 3: 1}
 
@@ -66,9 +67,9 @@
 
 def body(
     total_patches,
-    angles_ref, positions_ref, normals_ref, areas_ref, pressure_ref, velocity_ref, targets_hbm,
+    angles_ref, positions_ref, normals_ref, areas_ref, pressure_hbm, velocity_hbm, targets_hbm,
     responses_ref, grads_ref,
-    targets_t, targets_ref, angle_rows, angle_cols, angle_perm, split_t, split_x, t_rows, t_cols, t_lhs, x_rhs, face_rows, weights,
+    pressure_ref, velocity_ref, targets_t, targets_ref, angle_rows, angle_cols, angle_perm, split_t, split_x, t_rows, t_cols, t_lhs, x_rhs, face_rows, weights,
     cos_a, sin_a, cos_b, sin_b,
     part_send, part_recv, part_own, row_own, row_send, row_recv, res_all, acc,
     half_send, half_recv, quarter_own, quarter_send, quarter_recv, grad_all,
@@ -103,8 +104,12 @@
     own_rows = TILES * OWN
     fetch = pltpu.make_async_copy(
         targets_hbm.at[:, pl.ds(pl.multiple_of(surf_index * own_rows, own_rows), own_rows)],
-        targets_t, local_sem,
+        targets_t, local_sem.at[0],
     )
+    fetch_p = pltpu.make_async_copy(pressure_hbm, pressure_ref, local_sem.at[1])
+    fetch_v = pltpu.make_async_copy(velocity_hbm, velocity_ref, local_sem.at[2])
+    fetch_p.start()
+    fetch_v.start()
     fetch.start()
 
     angle_rows[...] = jnp.zeros_like(angle_rows)
@@ -139,6 +144,8 @@
     face_rows[3:4, :] = scale_row
     face_cols = face_rows[...].T
     scale_col = face_cols[:, 3:4]
+    fetch_p.wait()
+    fetch_v.wait()
     weighted_p = (pressure_ref[...].astype(F32) * scale_col).astype(BF).astype(F32)
     weighted_v = (velocity_ref[...].astype(F32) * scale_col).astype(BF).astype(F32)
     cases = weighted_p.shape[1] // 2
@@ -264,7 +271,7 @@
             total = total + part_recv[a_rows(q, e), :].astype(F32)
         row_own[rows, :] = total
         row_send[rows, :] = total.astype(BF)
-        for e in range(1, NZ):
+        for e in FAR_FIRST:
             b_copy(q, e).start()
 
     def make_residual(q):
@@ -281,13 +288,13 @@
         weight = (magnitude - targets_ref[out_rows, :]) / jnp.maximum(magnitude, FLOOR)
         residual = jnp.concatenate([weight * real, weight * imag], axis=1).astype(BF)
         res_all[pl.ds(pl.multiple_of(q * ROWS + OURS * SUB + z * OWN, OWN), OWN), :] = residual
-        for e in range(1, NZ):
+        for e in FAR_FIRST:
             d_copy(q, e).start()
 
     def share_over_y(q):
         for e in range(1, NZ):
             d_copy(q, e, came=True).wait_recv()
-        for e in range(1, NY):
+        for e in (2, 1, 3):
             e_copy(q, e).start()
 
     def adjoint_sides(q, parity):
@@ -336,9 +343,9 @@
         when(make_residual, 3)
         when(step_2, 0)
         when(step_3, 0)
-        when(share_over_y, 4)
         when(sum_over_y, 1)
         pl.when(it >= 6)(lambda: adjoint_tile(it - 6))
+        when(share_over_y, 4)
         return carry
 
     lax.fori_loop(0, TILES + 5, step, 0)
@@ -413,6 +420,15 @@
                 half_send[:, columns] = grad.astype(BF)
 
         g_copy(n).start()
+    def drain(q, carry):
+        for e in range(1, NY):
+            a_copy(q, e).wait_send()
+            e_copy(q, e).wait_send()
+        for e in range(1, NZ):
+            b_copy(q, e).wait_send()
+            d_copy(q, e).wait_send()
+        return carry
+
     for n, columns in enumerate(cuts):
         g_copy(n).wait_recv()
         chip = quarter_own[:, columns] + half_recv[:, columns].astype(F32)
@@ -420,6 +436,7 @@
         quarter_send[:, columns] = chip.astype(BF)
         for e in (2, 1, 3):
             h_copy(n, e).start()
+    lax.fori_loop(0, TILES, drain, 0)
     for n, columns in enumerate(cuts):
         total = quarter_own[pl.ds(pl.multiple_of(x * share, share), share), columns]
         for e in range(1, NX):
@@ -431,32 +448,22 @@
             k_copy(n, e).start()
         m_copy(n, 0).start()
     for n in range(2):
+        g_copy(n).wait_send()
+        for e in range(1, NX):
+            h_copy(n, e).wait_send()
+    for n in range(2):
         for e in (1, 3, 2):
             k_copy(n, e, came=True).wait_recv()
             m_copy(n, e).start()
     for n in range(2):
+        for e in range(1, NX):
+            k_copy(n, e).wait_send()
         for e in range(NX):
             m_copy(n, e, came=True).wait_recv()
     grads_ref[...] = grad_all[...]
-
     for n in range(2):
-        g_copy(n).wait_send()
-        for e in range(1, NX):
-            h_copy(n, e).wait_send()
-            k_copy(n, e).wait_send()
         for e in range(NX):
             m_copy(n, e).wait_send()
-
-    def drain(q, carry):
-        for e in range(1, NY):
-            a_copy(q, e).wait_send()
-            e_copy(q, e).wait_send()
-        for e in range(1, NZ):
-            b_copy(q, e).wait_send()
-            d_copy(q, e).wait_send()
-        return carry
-
-    lax.fori_loop(0, TILES, drain, 0)
 
 
 def finish(responses_ref, grads_ref, out_ref, grad_p_ref, grad_v_ref):
@@ -482,9 +489,11 @@
             jax.ShapeDtypeStruct((dirs // owners, half), F32),
             jax.ShapeDtypeStruct((2 * half, patches), BF),
         ),
-        in_specs=[vmem] * 6 + [pl.BlockSpec(memory_space=pl.ANY)],
+        in_specs=[vmem] * 4 + [pl.BlockSpec(memory_space=pl.ANY)] * 3,
         out_specs=(vmem, vmem),
         scratch_shapes=[
+            pltpu.VMEM((patches, half), BF),
+            pltpu.VMEM((patches, half), BF),
             pltpu.VMEM((cases, TILES * OWN), F32),
             pltpu.VMEM((TILES * OWN, cases), F32),
             pltpu.VMEM((8, dirs), F32),
@@ -516,7 +525,7 @@
             pltpu.VMEM((half, patches), BF),
             pltpu.VMEM((half // NX * (NX - 1), patches), BF),
             pltpu.VMEM((2 * half, patches), BF),
-            dma,
+            dma((3,)),
             dma((TILES * (NY - 1),)), dma((TILES * (NY - 1),)),
             dma((TILES * (NZ - 1),)), dma((TILES * (NZ - 1),)),
             dma((TILES * (NZ - 1),)), dma((TILES * (NZ - 1),)),

time: 64.2 us -> 63 us (0.981)
  Pallas kernels: 63.4 us -> 62.2 us
    pallas_call x1, Pallas kernels: 61.3 us -> 60.1 us  [shards(): pl.pallas_call(functools.partial(body, total_patches), out_shape=(jax.Sha...]
where the time goes in v4:
time: 63 us; the launch traced here: 62.8 us
  Pallas kernels  62.2 us (99%)
  between operations  0.64 us (1%)
    pallas_call x1, Pallas kernels, shards(): pl.pallas_call(functools.partial(body, total_patches), out_shape=(jax.Sha...  60.1 us
    pallas_call x1, Pallas kernels, shards(): pl.pallas_call(finish, out_shape=(jax.ShapeDtypeStruct((dirs // owners, h...  2.08 us

profile of v4, /device:TPU:1, one launch (start us, length us, event | category | flops | bytes accessed | tf_op | source)
XLA Modules:
  0.0 62.8 jit_solution(10362125054828641295)
XLA Ops:
  0.6 60.1 %shard_map.94 = (f32[128,128]{1,0:T(8,128)}, bf16[256,768]{1,0:T(8,128)(2,1)}) custom-call(f32[2,4096]{1,0:T(2,128)} %angles_ref.1, f32[3,768]{1,0:T(4,128)} %positions_ref.1, f32[2,768]{1,0:T(2,128)} %normals_ref.1, f32[6,128]{1,0:T(8,128)} %bitcast.3, bf16[768,128]{1,0:T(8,128)(2,1)} %pressure_hbm.1, bf16[768,128]{1,0:T(8,128)(2,1)} %velocity_hbm.1, ...), custom_call_target="tpu_custom_call" | custom-call | tf_op jit(solution)/shard_map/pallas_call | solution.py:486
  60.8 2.1 %shard_map.95 = (f32[128,128]{1,0:T(8,128)}, f32[768,128]{1,0:T(8,128)}, f32[768,128]{1,0:T(8,128)}) custom-call(f32[128,128]{1,0:T(8,128)} %get-tuple-element.5.responses_ref, bf16[256,768]{1,0:T(8,128)(2,1)} %get-tuple-element.6.grads_ref), custom_call_target="tpu_custom_call" | custom-call | tf_op jit(solution)/shard_map/pallas_call | solution.py:545

commit v5 on v4

--- a/solution.py
+++ b/solution.py
@@ -344,8 +344,8 @@
         when(step_2, 0)
         when(step_3, 0)
         when(sum_over_y, 1)
+        when(share_over_y, 4)
         pl.when(it >= 6)(lambda: adjoint_tile(it - 6))
-        when(share_over_y, 4)
         return carry
 
     lax.fori_loop(0, TILES + 5, step, 0)

time: 63 us -> 62 us (0.984)
  Pallas kernels: 62.2 us -> 61.2 us
    pallas_call x1, Pallas kernels: 60.1 us -> 59.1 us  [shards(): pl.pallas_call(functools.partial(body, total_patches), out_shape=(jax.Sha...]
where the time goes in v5:
time: 62 us; the launch traced here: 61.8 us
  Pallas kernels  61.2 us (99%)
  between operations  0.64 us (1%)
    pallas_call x1, Pallas kernels, shards(): pl.pallas_call(functools.partial(body, total_patches), out_shape=(jax.Sha...  59.1 us
    pallas_call x1, Pallas kernels, shards(): pl.pallas_call(finish, out_shape=(jax.ShapeDtypeStruct((dirs // owners, h...  2.08 us

profile of v5, /device:TPU:1, one launch (start us, length us, event | category | flops | bytes accessed | tf_op | source)
XLA Modules:
  0.0 61.8 jit_solution(18028917682302636518)
XLA Ops:
  0.6 59.1 %shard_map.94 = (f32[128,128]{1,0:T(8,128)}, bf16[256,768]{1,0:T(8,128)(2,1)}) custom-call(f32[2,4096]{1,0:T(2,128)} %angles_ref.1, f32[3,768]{1,0:T(4,128)} %positions_ref.1, f32[2,768]{1,0:T(2,128)} %normals_ref.1, f32[6,128]{1,0:T(8,128)} %bitcast.3, bf16[768,128]{1,0:T(8,128)(2,1)} %pressure_hbm.1, bf16[768,128]{1,0:T(8,128)(2,1)} %velocity_hbm.1, ...), custom_call_target="tpu_custom_call" | custom-call | tf_op jit(solution)/shard_map/pallas_call | solution.py:486
  59.7 2.1 %shard_map.95 = (f32[128,128]{1,0:T(8,128)}, f32[768,128]{1,0:T(8,128)}, f32[768,128]{1,0:T(8,128)}) custom-call(f32[128,128]{1,0:T(8,128)} %get-tuple-element.5.responses_ref, bf16[256,768]{1,0:T(8,128)(2,1)} %get-tuple-element.6.grads_ref), custom_call_target="tpu_custom_call" | custom-call | tf_op jit(solution)/shard_map/pallas_call | solution.py:545

commit v6 on v5

--- a/solution.py
+++ b/solution.py
@@ -352,7 +352,7 @@
 
     half = 2 * cases
     share = half // NX
-    cuts = (slice(0, 512), slice(512, patches))
+    cuts = (slice(0, 256), slice(256, patches))
     last = TILES - 1
 
     def gradient(which, columns):

time: 62 us -> 61.5 us (level)
  no operation moved by 1% of the time
where the time goes in v6:
time: 61.5 us; the launch traced here: 61.3 us
  Pallas kernels  60.7 us (99%)
  between operations  0.64 us (1%)
    pallas_call x1, Pallas kernels, shards(): pl.pallas_call(functools.partial(body, total_patches), out_shape=(jax.Sha...  58.6 us
    pallas_call x1, Pallas kernels, shards(): pl.pallas_call(finish, out_shape=(jax.ShapeDtypeStruct((dirs // owners, h...  2.08 us

profile of v6, /device:TPU:1, one launch (start us, length us, event | category | flops | bytes accessed | tf_op | source)
XLA Modules:
  0.0 61.3 jit_solution(12376704714656438027)
XLA Ops:
  0.6 58.6 %shard_map.94 = (f32[128,128]{1,0:T(8,128)}, bf16[256,768]{1,0:T(8,128)(2,1)}) custom-call(f32[2,4096]{1,0:T(2,128)} %angles_ref.1, f32[3,768]{1,0:T(4,128)} %positions_ref.1, f32[2,768]{1,0:T(2,128)} %normals_ref.1, f32[6,128]{1,0:T(8,128)} %bitcast.3, bf16[768,128]{1,0:T(8,128)(2,1)} %pressure_hbm.1, bf16[768,128]{1,0:T(8,128)(2,1)} %velocity_hbm.1, ...), custom_call_target="tpu_custom_call" | custom-call | tf_op jit(solution)/shard_map/pallas_call | solution.py:486
  59.3 2.1 %shard_map.95 = (f32[128,128]{1,0:T(8,128)}, f32[768,128]{1,0:T(8,128)}, f32[768,128]{1,0:T(8,128)}) custom-call(f32[128,128]{1,0:T(8,128)} %get-tuple-element.5.responses_ref, bf16[256,768]{1,0:T(8,128)(2,1)} %get-tuple-element.6.grads_ref), custom_call_target="tpu_custom_call" | custom-call | tf_op jit(solution)/shard_map/pallas_call | solution.py:545
